TPU v7x, 512 devices: a whole 4x8x8 slice. The times are simulated.
512 devices in a mesh: dp: 2 (over core), row: 64 (over z, y), col: 4 (over x).
Axes of the slice: x: 4, y: 8, z: 8, core: 2. Of those that a mesh axis runs over, the one named last changes fastest.
Arguments:
- grad_in: bfloat16 [2, 4096, 16384], P('dp', 'row', 'col'), may hold values from -50 to 50
- grad_out: bfloat16 [2, 16384, 4096], P('dp', 'row', 'col'), may hold values from -50 to 50
- rows_in: float32 [4096], P('row'), may hold values from 0.05 to 0.5
- cols_in: float32 [16384], P('col'), may hold values from 0.05 to 0.5
- rows_out: float32 [16384], P('row'), may hold values from 0.05 to 0.5
- cols_out: float32 [4096], P('col'), may hold values from 0.05 to 0.5
Outputs:
- update_in: float32 [4096, 16384], P('row', 'col')
- update_out: float32 [16384, 4096], P('row', 'col')
- rows_in_new: float32 [4096], P('row')
- cols_in_new: float32 [16384], P('col')
- rows_out_new: float32 [16384], P('row')
- cols_out_new: float32 [4096], P('col')
All inputs are finite; a program needn't handle non-finite values.
Results may differ from a plain program's by a relative error of at most 0.00045.
Values sent between devices are 32-bit elements; how exact they have to be, the bound alone decides.
No kernel may reach another device: no remote copies, remote signals or barrier semaphores. Data moves between devices by JAX's collectives and lax.ppermute only.
A program may use at most 64 MiB of HBM per device.

v0:
```python
import jax
import jax.numpy as jnp
from jax import lax
from jax.sharding import PartitionSpec as P

D = 4096
FF = 16384


EPSILON = 1e-30
DECAY = 1.0 - 100.0 ** (-0.8)


def per_device(grad_in, grad_out, rows_in, cols_in, rows_out, cols_out):
    term_in = grad_in[0].astype(jnp.float32)
    term_out = grad_out[0].astype(jnp.float32)
    summed_in, summed_out = lax.psum((term_in, term_out), "dp")
    square_in = summed_in * summed_in + EPSILON
    square_out = summed_out * summed_out + EPSILON
    rowsum_in, rowsum_out = lax.psum(
        (jnp.sum(square_in, axis=1), jnp.sum(square_out, axis=1)), "col"
    )
    colsum_in, colsum_out = lax.psum(
        (jnp.sum(square_in, axis=0), jnp.sum(square_out, axis=0)), "row"
    )
    rows_new_in = DECAY * rows_in + (1.0 - DECAY) * (rowsum_in / FF)
    cols_part_in = DECAY * cols_in + (1.0 - DECAY) * (colsum_in / D)
    rows_new_out = DECAY * rows_out + (1.0 - DECAY) * (rowsum_out / D)
    cols_part_out = DECAY * cols_out + (1.0 - DECAY) * (colsum_out / FF)
    scaled_in = summed_in * lax.rsqrt(rows_new_in)[:, None] * lax.rsqrt(cols_part_in)[None, :]
    scaled_out = summed_out * lax.rsqrt(rows_new_out)[:, None] * lax.rsqrt(cols_part_out)[None, :]
    local = (jnp.sum(scaled_in * scaled_in), jnp.sum(scaled_out * scaled_out))
    energy_in, energy_out = lax.psum((local[0], local[1]), ("row", "col"))
    ratio_in = jnp.sqrt(energy_in / (D * FF))
    ratio_out = jnp.sqrt(energy_out / (D * FF))
    update_in = scaled_in / jnp.maximum(1.0, ratio_in)
    update_out = scaled_out / jnp.maximum(1.0, ratio_out)
    return (update_in, update_out, rows_new_in, cols_part_in, rows_new_out, cols_part_out)


def solution(mesh):
    return jax.shard_map(
        per_device,
        mesh=mesh,
        in_specs=(
            P("dp", "row", "col"),
            P("dp", "row", "col"),
            P("row"),
            P("col"),
            P("row"),
            P("col"),
        ),
        out_specs=(P("row", "col"), P("row", "col"), P("row"), P("col"), P("row"), P("col")),
        check_vma=False,
    )
```

profile of v0, /device:TPU:2, one launch (start us, length us, event | category | flops | bytes accessed | tf_op | source)
XLA Modules:
  0.0 1046.8 jit_solution(11456601599323191503)
XLA Ops:
  7.2 0.0 copy-start.2
  7.2 0.0 all-reduce.6.cloned.1.call-start
  7.2 2.1 bitcast_convert_fusion.1
  9.4 1.1 bitcast_convert_fusion
  10.4 0.0 all-reduce.6.cloned.1.call-update
  10.5 43.4 %all-reduce.6.cloned.1.call-done = (f32[64,4096]{1,0:T(8,128)}, f32[256,1024]{1,0:T(8,128)}) async-done(((f32[64,4096]{1,0:T(8,128)}, f32[256,1024]{1,0:T(8,128)}), (f32[64,4096]{1,0:T(8,128)}, f32[256,1024]{1,0:T(8,128)})) %all-reduce.6.cloned.1.call-update) | async-done | bytes 2097168 | tf_op jit(solution)/shard_map/psum | solution.py:17
  53.9 1.6 fusion.4
  55.4 0.0 copy-done.1
  55.4 0.0 copy-start.4
  55.4 0.0 copy-start
  55.4 0.2 fusion.1
  55.7 9.4 all-reduce.2
  65.1 0.7 copy-done.6
  65.8 0.5 fusion.8
  66.3 0.7 copy-done.5
  66.9 0.6 fusion.6
  67.5 279.6 %all-reduce.1 = (f32[4096]{0:T(1024)S(1)}, f32[1024]{0:T(1024)S(1)}) all-reduce(f32[4096]{0:T(1024)S(1)} %get-tuple-element.9, f32[1024]{0:T(1024)S(1)} %get-tuple-element.7), channel_id=1, replica_groups=mesh['dp'=2,'row'=64,'col'=4] {'row'}, use_global_device_ids=true, to_apply=%region_4.0 | all-reduce | flops 5120 | bytes 40960 | tf_op jit(solution)/shard_map/psum | solution.py:23
  347.1 0.6 fusion.7
  347.7 0.6 fusion.9
  348.3 0.9 multiply_reduce_fusion.1
  349.3 1.0 multiply_reduce_fusion
  350.3 686.0 %all-reduce = (f32[]{:T(128)}, f32[]{:T(128)}) all-reduce(f32[]{:T(128)} %multiply_reduce_fusion.1, f32[]{:T(128)} %multiply_reduce_fusion), channel_id=1, replica_groups=mesh['dp'=2,'row'=64,'col'=4] {'row','col'}, use_global_device_ids=true, to_apply=%region_6.0 | all-reduce | flops 2 | bytes 16 | tf_op jit(solution)/shard_map/psum | solution.py:33
  1037.6 1.2 fusion.2
  1038.8 1.2 fusion.5
  (8 shorter events, 0.0 us)
Async XLA Ops:
  7.2 2.2 copy-start.2
  7.2 46.7 %all-reduce.6.cloned.1.call-start = ((), (), s32[]{:S(2)}) async-start(), calls=%async_computation | async-start | bytes 4194304 | tf_op jit(solution)/shard_map/psum | solution.py:17
  53.9 1.6 copy-start.1
  55.4 291.7 %copy-start.4 = (f32[1024]{0:T(1024)S(1)}, f32[1024]{0:T(1024)}, u32[]{:S(2)}) copy-start(f32[1024]{0:T(1024)} %param.11) | copy-start | bytes 12292
  55.4 293.8 %copy-start = (f32[256,1024]{1,0:T(8,128)S(1)}, f32[256,1024]{1,0:T(8,128)}, u32[]{:S(2)}) copy-start(f32[256,1024]{1,0:T(8,128)} %get-tuple-element.17) | copy-start | bytes 3145732
  65.1 0.7 copy-start.6
  66.3 0.7 copy-start.5
  67.5 280.2 %copy-start.3 = (f32[4096]{0:T(1024)S(1)}, f32[4096]{0:T(1024)}, u32[]{:S(2)}) copy-start(f32[4096]{0:T(1024)} %param.9) | copy-start | bytes 49156
Sparse Core Ops, SparseCore 0:
  11.5 42.3 all-reduce.5
where the time goes:
time: 1050 us
  blocking collectives  975 us (93%)
  waiting for transfers between devices  43.4 us (4%)
  between operations  15.4 us (1%)
  other arithmetic  11.6 us (1%)
    psum x1, blocking collectives, per_device(): energy_in, energy_out = lax.psum((local[0], local[1]), ('row', 'col'))  686 us
    psum x1, blocking collectives, per_device(): lax.psum((jnp.sum(square_in, axis=0), jnp.sum(square_out, axis=0)), 'row')  280 us
    psum x1, waiting for transfers between devices, per_device(): summed_in, summed_out = lax.psum((term_in, term_out), 'dp')  43.4 us
  transfers between devices with their start and end apart: 1, of which 1 were waited for; matrix products, arithmetic and copies ran while one was open for 0% of the time, Pallas kernels for 0%

commit v1 on v0

v1 whole, which is shorter than its diff:
```python
import jax
import jax.numpy as jnp
from jax import lax
from jax.experimental import pallas as pl
from jax.experimental.pallas import tpu as pltpu
from jax.sharding import Mesh, PartitionSpec as P

D = 4096
FF = 16384

EPSILON = 1e-30
DECAY = 1.0 - 100.0 ** (-0.8)

ROWS_IN, COLS_IN = 64, 4096
ROWS_OUT, COLS_OUT = 256, 1024
HALF_IN, HALF_OUT = COLS_IN // 2, COLS_OUT // 2
PACK = (128, 2048)
BLOCKS = ROWS_OUT // 64
TILES_IN = HALF_IN // 128
TILES_OUT = HALF_OUT // 128

F32 = jnp.float32
VMEM = pl.BlockSpec(memory_space=pltpu.VMEM)
HBM = pl.BlockSpec(memory_space=pl.ANY)
PARAMS = pltpu.CompilerParams(vmem_limit_bytes=16 * 1024 * 1024)


def lanes(tile):
    return pl.ds(tile * 128, 128)


def widen_kernel(other, grad_in, grad_out, packed, buf_in, buf_out, sems):
    half = lax.axis_index("dp")
    if other:
        half = 1 - half
    copy_in = pltpu.make_async_copy(
        grad_in.at[:, pl.ds(pl.multiple_of(half * HALF_IN, 128), HALF_IN)], buf_in, sems.at[0]
    )
    copy_out = pltpu.make_async_copy(
        grad_out.at[:, pl.ds(pl.multiple_of(half * HALF_OUT, 128), HALF_OUT)], buf_out, sems.at[1]
    )
    copy_in.start()
    copy_out.start()
    copy_in.wait()
    packed[0:64, :] = buf_in[...].astype(F32)
    copy_out.wait()
    for k in range(BLOCKS):
        packed[64:128, pl.ds(k * HALF_OUT, HALF_OUT)] = buf_out[pl.ds(64 * k, 64), :].astype(F32)


def widen(other, grad_in, grad_out):
    return pl.pallas_call(
        lambda *refs: widen_kernel(other, *refs),
        out_shape=jax.ShapeDtypeStruct(PACK, F32),
        in_specs=[HBM, HBM],
        out_specs=VMEM,
        scratch_shapes=[
            pltpu.VMEM((ROWS_IN, HALF_IN), jnp.bfloat16),
            pltpu.VMEM((ROWS_OUT, HALF_OUT), jnp.bfloat16),
            pltpu.SemaphoreType.DMA((2,)),
        ],
        compiler_params=PARAMS,
        name="widen_other" if other else "widen_own",
    )(grad_in, grad_out)


def rows_kernel(own, received, summed, row_sums):
    def lane_partial(row, tiles):
        total = None
        for tile in tiles:
            value = own[pl.ds(row, 64), lanes(tile)] + received[pl.ds(row, 64), lanes(tile)]
            summed[pl.ds(row, 64), lanes(tile)] = value
            square = value * value
            total = square if total is None else total + square
        return total

    def to_lanes(upper, lower):
        return jnp.sum(jnp.concatenate([upper, lower], axis=0).T, axis=0, keepdims=True)

    part = lane_partial(0, range(TILES_IN))
    vectors = [to_lanes(part, jnp.zeros_like(part))]
    for pair in range(BLOCKS // 2):
        upper, lower = (
            lane_partial(64, range(k * TILES_OUT, (k + 1) * TILES_OUT)) for k in (2 * pair, 2 * pair + 1)
        )
        vectors.append(to_lanes(upper, lower))
    for at, vector in enumerate(vectors):
        for peer in range(8):
            row_sums[peer, :, lanes(at)] = vector


def row_sums_of(own, received):
    return pl.pallas_call(
        rows_kernel,
        out_shape=(jax.ShapeDtypeStruct(PACK, F32), jax.ShapeDtypeStruct((8, 1, 384), F32)),
        in_specs=[VMEM, VMEM],
        out_specs=(VMEM, VMEM),
        compiler_params=PARAMS,
        name="row_sums",
    )(own, received)


def columns_kernel(row_sums, rows_in, rows_out, summed, scaled, row_scale, new_in, new_out, sends):
    total = jnp.sum(row_sums[...], axis=0)
    fresh_in = DECAY * rows_in[...] + (1.0 - DECAY) * (total[:, 0:64] * (1.0 / FF) + EPSILON)
    fresh_out = DECAY * rows_out[...] + (1.0 - DECAY) * (total[:, 128:384] * (1.0 / D) + EPSILON)
    new_in[...] = fresh_in
    new_out[...] = fresh_out
    root_in = lax.rsqrt(fresh_in)
    root_out = lax.rsqrt(fresh_out)

    def to_rows(vector):
        return jnp.broadcast_to(vector, (128, 128)).T

    row_scale[0:64, :] = to_rows(jnp.concatenate([root_in, root_in], axis=1))[0:64, :]
    row_scale[64:192, :] = to_rows(root_out[:, 0:128])
    row_scale[192:320, :] = to_rows(root_out[:, 128:256])

    def column(row, scale_row, tile):
        value = summed[pl.ds(row, 64), lanes(tile)]
        weighted = value * row_scale[pl.ds(scale_row, 64), :]
        scaled[pl.ds(row, 64), lanes(tile)] = weighted
        return (
            jnp.sum((value * value).reshape(8, 8, 128), axis=0),
            jnp.sum((weighted * weighted).reshape(8, 8, 128), axis=0),
        )

    def fold(value):
        return jnp.sum(value, axis=0, keepdims=True)

    def send(chunk, at, vector):
        for peer in range(8):
            sends[chunk * 8 + peer, :, lanes(at)] = vector

    for tile in range(TILES_IN):
        plain, weighted = column(0, 0, tile)
        send(tile // 2, tile % 2, fold(plain))
        send(tile // 2, 2 + tile % 2, fold(weighted))
    lane = lax.broadcasted_iota(jnp.int32, (1, 128), 1)
    for tile in range(TILES_OUT):
        plain, weighted = column(64, 64, tile)
        for k in range(1, BLOCKS):
            more = column(64, 64 + 64 * k, k * TILES_OUT + tile)
            plain, weighted = plain + more[0], weighted + more[1]
        plain, weighted = fold(plain), fold(weighted)
        send(2 * tile, 4, jnp.where(lane < 64, plain, pltpu.roll(weighted, 64, 1)))
        send(2 * tile + 1, 4, jnp.where(lane < 64, pltpu.roll(plain, 64, 1), weighted))


def column_sums_of(row_sums, rows_in, rows_out, summed):
    return pl.pallas_call(
        columns_kernel,
        out_shape=(
            jax.ShapeDtypeStruct(PACK, F32),
            jax.ShapeDtypeStruct((320, 128), F32),
            jax.ShapeDtypeStruct((1, ROWS_IN), F32),
            jax.ShapeDtypeStruct((1, ROWS_OUT), F32),
            jax.ShapeDtypeStruct((64, 1, 640), F32),
        ),
        in_specs=[VMEM] * 4,
        out_specs=(VMEM,) * 5,
        compiler_params=PARAMS,
        name="column_sums",
    )(row_sums, rows_in, rows_out, summed)


def factors_kernel(sums, cols_in, cols_out, sends):
    owner = lax.axis_index("dp") * 8 + lax.axis_index("z")
    total = jnp.sum(sums[...], axis=0)
    lane = lax.broadcasted_iota(jnp.int32, (1, 128), 1)
    new_in = DECAY * cols_in[owner] + (1.0 - DECAY) * (total[:, 0:256] * (1.0 / D) + EPSILON)
    energy_in = jnp.sum(total[:, 256:512] / new_in, axis=1, keepdims=True)
    mixed = total[:, 512:640]
    old_out = cols_out[owner // 2]
    old_out = jnp.where(owner % 2 == 1, pltpu.roll(old_out, 64, 1), old_out)
    new_out = DECAY * old_out + (1.0 - DECAY) * (mixed * (1.0 / FF) + EPSILON)
    weighted = jnp.where(lane < 64, pltpu.roll(mixed, 64, 1) / new_out, 0.0)
    energy_out = jnp.sum(weighted, axis=1, keepdims=True)
    last = jnp.where(lane < 64, new_out, jnp.where(lane < 96, energy_in, energy_out))
    for peer in range(64):
        sends[peer, :, 0:256] = new_in
        sends[peer, :, 256:384] = last


def factors_of(sums, cols_in, cols_out):
    return pl.pallas_call(
        factors_kernel,
        out_shape=jax.ShapeDtypeStruct((64, 1, 384), F32),
        in_specs=[VMEM] * 3,
        out_specs=VMEM,
        compiler_params=PARAMS,
        name="column_factors",
    )(sums, cols_in, cols_out)


def update_kernel(
    factors, scaled, row_scale, other, received, update_in, update_out, cols_in, cols_out, buf_in, buf_out, sems
):
    own_half = lax.axis_index("dp")
    my_x = lax.axis_index("x")
    lane = lax.broadcasted_iota(jnp.int32, (1, 128), 1)
    energies = jnp.sum(factors[:, :, 256:384], axis=0)

    def limit(at):
        energy = jnp.sum(jnp.where(lane == at, energies, 0.0), axis=1, keepdims=True)
        return 1.0 / jnp.maximum(1.0, jnp.sqrt(energy * (1.0 / (D * FF))))

    limit_in, limit_out = limit(64), limit(96)

    def factor_in(half, tile):
        return factors[(half * 8 + tile // 2) * 4 + my_x, :, lanes(tile % 2)]

    def factor_out(half, tile):
        left = factors[(half * 8 + 2 * tile) * 4 + my_x, :, lanes(2)]
        right = factors[(half * 8 + 2 * tile + 1) * 4 + my_x, :, lanes(2)]
        return jnp.where(lane < 64, left, pltpu.roll(right, 64, 1))

    copies = []
    for which in range(2):
        half = own_half if which == 0 else 1 - own_half

        def value(row, scale_row, tile):
            if which == 0:
                return scaled[pl.ds(row, 64), lanes(tile)]
            both = other[pl.ds(row, 64), lanes(tile)] + received[pl.ds(row, 64), lanes(tile)]
            return both * row_scale[pl.ds(scale_row, 64), :]

        for tile in range(TILES_IN):
            factor = factor_in(half, tile)
            buf_in[which, :, lanes(tile)] = value(0, 0, tile) * (lax.rsqrt(factor) * limit_in)
        copy = pltpu.make_async_copy(
            buf_in.at[which],
            update_in.at[:, pl.ds(pl.multiple_of(half * HALF_IN, 128), HALF_IN)],
            sems.at[2 * which],
        )
        copy.start()
        copies.append(copy)
        for tile in range(TILES_OUT):
            scale = lax.rsqrt(factor_out(half, tile)) * limit_out
            for k in range(BLOCKS):
                buf_out[which, pl.ds(64 * k, 64), lanes(tile)] = (
                    value(64, 64 + 64 * k, k * TILES_OUT + tile) * scale
                )
        copy = pltpu.make_async_copy(
            buf_out.at[which],
            update_out.at[:, pl.ds(pl.multiple_of(half * HALF_OUT, 128), HALF_OUT)],
            sems.at[2 * which + 1],
        )
        copy.start()
        copies.append(copy)
    for half in range(2):
        for tile in range(TILES_IN):
            cols_in[pl.ds(half * TILES_IN + tile, 1), :] = factor_in(half, tile)
        for tile in range(TILES_OUT):
            cols_out[pl.ds(half * TILES_OUT + tile, 1), :] = factor_out(half, tile)
    for copy in copies:
        copy.wait()


def update_of(factors, scaled, row_scale, other, received):
    return pl.pallas_call(
        update_kernel,
        out_shape=(
            jax.ShapeDtypeStruct((ROWS_IN, COLS_IN), F32),
            jax.ShapeDtypeStruct((ROWS_OUT, COLS_OUT), F32),
            jax.ShapeDtypeStruct((COLS_IN // 128, 128), F32),
            jax.ShapeDtypeStruct((COLS_OUT // 128, 128), F32),
        ),
        in_specs=[VMEM] * 5,
        out_specs=(HBM, HBM, VMEM, VMEM),
        scratch_shapes=[
            pltpu.VMEM((2, ROWS_IN, HALF_IN), F32),
            pltpu.VMEM((2, ROWS_OUT, HALF_OUT), F32),
            pltpu.SemaphoreType.DMA((4,)),
        ],
        compiler_params=PARAMS,
        name="update",
    )(factors, scaled, row_scale, other, received)


def per_device(grad_in, grad_out, rows_in, cols_in, rows_out, cols_out):
    grad_in, grad_out = grad_in[0], grad_out[0]
    swap = [(0, 1), (1, 0)]
    other = widen(True, grad_in, grad_out)
    arrived_own = lax.ppermute(other, "dp", swap)
    own = widen(False, grad_in, grad_out)
    arrived_other = lax.ppermute(own, "dp", swap)

    summed, row_sums = row_sums_of(own, arrived_own)
    row_sums = lax.all_to_all(row_sums, ("dp", "x"), 0, 0)
    scaled, row_scale, new_rows_in, new_rows_out, sums = column_sums_of(
        row_sums, rows_in.reshape(1, ROWS_IN), rows_out.reshape(1, ROWS_OUT), summed
    )
    sums = lax.all_to_all(sums, ("z", "y"), 0, 0)
    factors = factors_of(sums, cols_in.reshape(16, 1, 256), cols_out.reshape(8, 1, 128))
    factors = lax.all_to_all(factors, ("dp", "z", "x"), 0, 0)
    update_in, update_out, new_cols_in, new_cols_out = update_of(
        factors, scaled, row_scale, other, arrived_other
    )
    return (
        update_in,
        update_out,
        new_rows_in.reshape(ROWS_IN),
        new_cols_in.reshape(COLS_IN),
        new_rows_out.reshape(ROWS_OUT),
        new_cols_out.reshape(COLS_OUT),
    )


def solution(mesh):
    fine = Mesh(mesh.devices.reshape(2, 8, 8, 4), ("dp", "z", "y", "x"))
    row = ("z", "y")
    return jax.shard_map(
        per_device,
        mesh=fine,
        in_specs=(
            P("dp", row, "x"),
            P("dp", row, "x"),
            P(row),
            P("x"),
            P(row),
            P("x"),
        ),
        out_specs=(P(row, "x"), P(row, "x"), P(row), P("x"), P(row), P("x")),
        check_vma=False,
    )
```

time: 1050 us -> 70.2 us (0.07)
  the two profiles are of different devices: /device:TPU:2 before, /device:TPU:1 now
where the time goes in v1:
time: 70.2 us; the launch traced here: 69.7 us
  blocking collectives  32 us (46%)
  starting transfers between devices  17.3 us (25%)
  waiting for transfers between devices  10.3 us (15%)
  local copies, waits for them, and re-layouts  4.96 us (7%)
  Pallas kernels  4.46 us (6%)
    all_to_all x1, blocking collectives, per_device(): sums = lax.all_to_all(sums, ('z', 'y'), 0, 0)  24.4 us
    all_to_all x1, waiting for transfers between devices, per_device(): factors = lax.all_to_all(factors, ('dp', 'z', 'x'), 0, 0)  10.1 us
    ppermute x1, starting transfers between devices, per_device(): arrived_own = lax.ppermute(other, 'dp', swap)  8.79 us
    all_to_all x1, blocking collectives, per_device(): row_sums = lax.all_to_all(row_sums, ('dp', 'x'), 0, 0)  7.62 us
    all_to_all x1, starting transfers between devices, per_device(): factors = lax.all_to_all(factors, ('dp', 'z', 'x'), 0, 0)  6.6 us
    unnamed x16, local copies, waits for them, and re-layouts  4.96 us
    pallas_call x1, Pallas kernels, update_of(): pl.pallas_call(update_kernel, out_shape=(jax.ShapeDtypeStruct((ROWS_IN, C...  2.17 us
    ppermute x1, starting transfers between devices, per_device(): arrived_other = lax.ppermute(own, 'dp', swap)  1.92 us
  transfers between devices with their start and end apart: 3, of which 2 were waited for; matrix products, arithmetic and copies ran while one was open for 0% of the time, Pallas kernels for 3%

profile of v1, /device:TPU:1, one launch (start us, length us, event | category | flops | bytes accessed | tf_op | source)
XLA Modules:
  0.0 69.7 jit_solution(4763050913220838108)
XLA Ops:
  0.6 0.0 copy-start
  0.6 1.0 %copy-done = bf16[1,64,4096]{2,1,0:T(8,128)(2,1)S(1)} copy-done((bf16[1,64,4096]{2,1,0:T(8,128)(2,1)S(1)}, bf16[1,64,4096]{2,1,0:T(8,128)(2,1)}, u32[]{:S(2)}) %copy-start) | copy-done | bytes 524312
  1.7 0.0 copy-start.1
  1.7 1.0 %copy-done.1 = bf16[1,256,1024]{2,1,0:T(8,128)(2,1)S(1)} copy-done((bf16[1,256,1024]{2,1,0:T(8,128)(2,1)S(1)}, bf16[1,256,1024]{2,1,0:T(8,128)(2,1)}, u32[]{:S(2)}) %copy-start.1) | copy-done | bytes 524312
  2.7 0.1 widen_other.1.other
  2.9 8.8 %collective-permute-start = (f32[128,2048]{1,0:T(8,128)S(1)}, f32[128,2048]{1,0:T(8,128)S(1)}, u32[]{:S(2)}, u32[]{:S(2)}) collective-permute-start(f32[128,2048]{1,0:T(8,128)S(1)} %widen_other.1.other), channel_id=1, source_target_pairs={{0,256},{256,0},{1,257},{257,1},{2,258},{258,2},{3,259},{259,3},{4... | collective-permute-start | bytes 3145736 | tf_op jit(solution)/shard_map/ppermute | solution.py:285
  11.6 0.1 widen_own.1.own
  11.8 1.9 %collective-permute-start.1 = (f32[128,2048]{1,0:T(8,128)S(1)}, f32[128,2048]{1,0:T(8,128)S(1)}, u32[]{:S(2)}, u32[]{:S(2)}) collective-permute-start(f32[128,2048]{1,0:T(8,128)S(1)} %widen_own.1.own), channel_id=1, source_target_pairs={{0,256},{256,0},{1,257},{257,1},{2,258},{258,2},{3,259},{259,3},{4... | collective-permute-start | bytes 3145736 | tf_op jit(solution)/shard_map/ppermute | solution.py:287
  13.7 0.2 collective-permute-done.received
  13.9 0.2 row_sums.1
  14.1 7.6 %all_to_all.15.row_sums = f32[8,1,384]{2,1,0:T(1,128)S(1)} all-to-all(f32[8,1,384]{2,1,0:T(1,128)S(1)} %get-tuple-element.17), channel_id=1, replica_groups=mesh['dp'=2,'z'=8,'y'=8,'x'=4] {'dp','x'}, dimensions={0} | all-to-all | bytes 24576 | tf_op jit(solution)/shard_map/all_to_all | solution.py:290
  21.8 0.7 copy-done.6
  22.4 0.0 copy-done.7
  22.4 0.9 %column_sums.1 = (f32[128,2048]{1,0:T(8,128)S(1)}, f32[320,128]{1,0:T(8,128)S(1)}, f32[1,64]{1,0:T(1,128)}, f32[1,256]{1,0:T(1,128)}, f32[64,1,640]{2,1,0:T(1,128)S(1)}) custom-call(f32[8,1,384]{2,1,0:T(1,128)S(1)} %all_to_all.15.row_sums, f32[1,64]{1,0:T(1,128)S(1)} %bitcast.17, f32[1,256]{1,0:T(1,128)S(1)} %bitcast.16, ...), custom_call_target="tpu_custom_call" | custom-call | tf_op jit(solution)/shard_map/column_sums/pallas_call | solution.py:151
  23.3 1.0 %copy-done.2 = f32[128,2048]{1,0:T(8,128)} copy-done((f32[128,2048]{1,0:T(8,128)}, f32[128,2048]{1,0:T(8,128)S(1)}, u32[]{:S(2)}) %copy-start.2) | copy-done | bytes 1048600
  24.3 24.4 %all_to_all.16.sums = f32[64,1,640]{2,1,0:T(1,128)S(1)} all-to-all(f32[64,1,640]{2,1,0:T(1,128)S(1)} %get-tuple-element.19), channel_id=1, replica_groups=mesh['dp'=2,'z'=8,'y'=8,'x'=4] {'z','y'}, dimensions={0} | all-to-all | bytes 327680 | tf_op jit(solution)/shard_map/all_to_all | solution.py:294
  48.7 0.0 copy-done.4
  48.7 0.0 copy-done.5
  48.7 0.9 %column_factors.1 = f32[64,1,384]{2,1,0:T(1,128)} custom-call(f32[64,1,640]{2,1,0:T(1,128)S(1)} %all_to_all.16.sums, f32[16,1,256]{2,1,0:T(1,128)S(1)} %bitcast.14, f32[8,1,128]{2,1,0:T(1,128)S(1)} %bitcast.15), custom_call_target="tpu_custom_call" | custom-call | tf_op jit(solution)/shard_map/column_factors/pallas_call | solution.py:186
  49.6 6.6 %all-to-all-start.2 = ((f32[64,1,384]{2,1,0:T(1,128)}), f32[64,1,384]{2,1,0:T(1,128)S(1)}, u32[]{:S(2)}, u32[]{:S(2)}) async-start(f32[64,1,384]{2,1,0:T(1,128)} %column_factors.1), calls=%async_computation.2 | async-start | bytes 196608 | tf_op jit(solution)/shard_map/all_to_all | solution.py:296
  56.2 0.0 collective-permute-done.1.received
  56.2 10.1 %all-to-all-done.2.factors = f32[64,1,384]{2,1,0:T(1,128)S(1)} async-done(((f32[64,1,384]{2,1,0:T(1,128)}), f32[64,1,384]{2,1,0:T(1,128)S(1)}, u32[]{:S(2)}, u32[]{:S(2)}) %all-to-all-start.2) | async-done | bytes 98336 | tf_op jit(solution)/shard_map/all_to_all | solution.py:296
  66.3 1.2 %copy-done.3 = f32[128,2048]{1,0:T(8,128)S(1)} copy-done((f32[128,2048]{1,0:T(8,128)S(1)}, f32[128,2048]{1,0:T(8,128)}, u32[]{:S(2)}) %copy-start.3) | copy-done | bytes 1048600
  67.5 2.2 %update.1 = (f32[64,4096]{1,0:T(8,128)}, f32[256,1024]{1,0:T(8,128)}, f32[32,128]{1,0:T(8,128)}, f32[8,128]{1,0:T(8,128)}) custom-call(f32[64,1,384]{2,1,0:T(1,128)S(1)} %all-to-all-done.2.factors, f32[128,2048]{1,0:T(8,128)S(1)} %copy-done.3, f32[320,128]{1,0:T(8,128)S(1)} %get-tuple-element.21.row_scale, f32[128,2048]{1,0:T(8,128)S(1)} %widen_other.1.other, ...), custom_call_target="tpu_custom_call" | custom-call | tf_op jit(solution)/shard_map/update/pallas_call | solution.py:261
  (6 shorter events, 0.0 us)
Async XLA Ops:
  0.6 1.0 %copy-start = (bf16[1,64,4096]{2,1,0:T(8,128)(2,1)S(1)}, bf16[1,64,4096]{2,1,0:T(8,128)(2,1)}, u32[]{:S(2)}) copy-start(bf16[1,64,4096]{2,1,0:T(8,128)(2,1)} %param.6) | copy-start | bytes 1572868
  1.7 1.0 %copy-start.1 = (bf16[1,256,1024]{2,1,0:T(8,128)(2,1)S(1)}, bf16[1,256,1024]{2,1,0:T(8,128)(2,1)}, u32[]{:S(2)}) copy-start(bf16[1,256,1024]{2,1,0:T(8,128)(2,1)} %param.7) | copy-start | bytes 1572868
  2.9 11.1 %collective-permute-start = (f32[128,2048]{1,0:T(8,128)S(1)}, f32[128,2048]{1,0:T(8,128)S(1)}, u32[]{:S(2)}, u32[]{:S(2)}) collective-permute-start(f32[128,2048]{1,0:T(8,128)S(1)} %widen_other.1.other), channel_id=1, source_target_pairs={{0,256},{256,0},{1,257},{257,1},{2,258},{258,2},{3,259},{259,3},{4... | collective-permute-start | bytes 3145736 | tf_op jit(solution)/shard_map/ppermute | solution.py:285
  11.8 44.4 %collective-permute-start.1 = (f32[128,2048]{1,0:T(8,128)S(1)}, f32[128,2048]{1,0:T(8,128)S(1)}, u32[]{:S(2)}, u32[]{:S(2)}) collective-permute-start(f32[128,2048]{1,0:T(8,128)S(1)} %widen_own.1.own), channel_id=1, source_target_pairs={{0,256},{256,0},{1,257},{257,1},{2,258},{258,2},{3,259},{259,3},{4... | collective-permute-start | bytes 3145736 | tf_op jit(solution)/shard_map/ppermute | solution.py:287
  21.7 0.7 copy-start.6
  21.8 0.7 copy-start.7
  23.3 1.0 %copy-start.2 = (f32[128,2048]{1,0:T(8,128)}, f32[128,2048]{1,0:T(8,128)S(1)}, u32[]{:S(2)}) copy-start(f32[128,2048]{1,0:T(8,128)S(1)} %get-tuple-element.20.scaled) | copy-start | bytes 3145732
  24.3 24.4 %copy-start.4 = (f32[4096]{0:T(1024)S(1)}, f32[4096]{0:T(1024)}, u32[]{:S(2)}) copy-start(f32[4096]{0:T(1024)} %param.9) | copy-start | bytes 49156
  24.3 24.4 %copy-start.5 = (f32[1024]{0:T(1024)S(1)}, f32[1024]{0:T(1024)}, u32[]{:S(2)}) copy-start(f32[1024]{0:T(1024)} %param.11) | copy-start | bytes 12292
  49.6 16.7 %all-to-all-start.2 = ((f32[64,1,384]{2,1,0:T(1,128)}), f32[64,1,384]{2,1,0:T(1,128)S(1)}, u32[]{:S(2)}, u32[]{:S(2)}) async-start(f32[64,1,384]{2,1,0:T(1,128)} %column_factors.1), calls=%async_computation.2 | async-start | bytes 196608 | tf_op jit(solution)/shard_map/all_to_all | solution.py:296
  66.3 1.2 %copy-start.3 = (f32[128,2048]{1,0:T(8,128)S(1)}, f32[128,2048]{1,0:T(8,128)}, u32[]{:S(2)}) copy-start(f32[128,2048]{1,0:T(8,128)} %copy-done.2) | copy-start | bytes 3145732

commit v2 on v1

--- a/solution.py
+++ b/solution.py
@@ -21,7 +21,7 @@
 
 F32 = jnp.float32
 VMEM = pl.BlockSpec(memory_space=pltpu.VMEM)
-HBM = pl.BlockSpec(memory_space=pl.ANY)
+HBM = pl.BlockSpec(memory_space=pltpu.HBM)
 PARAMS = pltpu.CompilerParams(vmem_limit_bytes=16 * 1024 * 1024)
 
 
@@ -29,39 +29,120 @@
     return pl.ds(tile * 128, 128)
 
 
-def widen_kernel(other, grad_in, grad_out, packed, buf_in, buf_out, sems):
-    half = lax.axis_index("dp")
-    if other:
-        half = 1 - half
+def widen_in(packed, block):
+    packed[0:64, :] = block[...].astype(F32)
+
+
+def widen_out(packed, block):
+    for k in range(BLOCKS):
+        packed[64:128, pl.ds(k * HALF_OUT, HALF_OUT)] = block[pl.ds(64 * k, 64), :].astype(F32)
+
+
+def fetch_kernel(
+    grad_in, grad_out, rows_in, rows_out, cols_in, cols_out,
+    other, own_in, own_out, rows_in_here, rows_out_here, cols_in_here, cols_out_here,
+    other_in, other_out, sems,
+):
+    own_half = lax.axis_index("dp")
+
+    def block_in(half):
+        return grad_in.at[:, pl.ds(pl.multiple_of(half * HALF_IN, 128), HALF_IN)]
+
+    def block_out(half):
+        return grad_out.at[:, pl.ds(pl.multiple_of(half * HALF_OUT, 128), HALF_OUT)]
+
+    pairs = (
+        (block_in(1 - own_half), other_in),
+        (block_out(1 - own_half), other_out),
+        (block_in(own_half), own_in),
+        (block_out(own_half), own_out),
+        (rows_in, rows_in_here),
+        (rows_out, rows_out_here),
+        (cols_in, cols_in_here),
+        (cols_out, cols_out_here),
+    )
+    copies = [pltpu.make_async_copy(src, dst, sems.at[at]) for at, (src, dst) in enumerate(pairs)]
+    for copy in copies:
+        copy.start()
+    copies[0].wait()
+    widen_in(other, other_in)
+    copies[1].wait()
+    widen_out(other, other_out)
+    for copy in copies[2:]:
+        copy.wait()
+
+
+def fetch(grad_in, grad_out, rows_in, rows_out, cols_in, cols_out):
+    return pl.pallas_call(
+        fetch_kernel,
+        out_shape=(
+            jax.ShapeDtypeStruct(PACK, F32),
+            jax.ShapeDtypeStruct((ROWS_IN, HALF_IN), jnp.bfloat16),
+            jax.ShapeDtypeStruct((ROWS_OUT, HALF_OUT), jnp.bfloat16),
+        )
+        + tuple(jax.ShapeDtypeStruct(x.shape, F32) for x in (rows_in, rows_out, cols_in, cols_out)),
+        in_specs=[HBM] * 6,
+        out_specs=(VMEM,) * 7,
+        scratch_shapes=[
+            pltpu.VMEM((ROWS_IN, HALF_IN), jnp.bfloat16),
+            pltpu.VMEM((ROWS_OUT, HALF_OUT), jnp.bfloat16),
+            pltpu.SemaphoreType.DMA((8,)),
+        ],
+        compiler_params=PARAMS,
+        name="fetch",
+    )(grad_in, grad_out, rows_in, rows_out, cols_in, cols_out)
+
+
+def widen_kernel(own_in, own_out, packed):
+    widen_in(packed, own_in)
+    widen_out(packed, own_out)
+
+
+def widen_own(own_in, own_out):
+    return pl.pallas_call(
+        widen_kernel,
+        out_shape=jax.ShapeDtypeStruct(PACK, F32),
+        in_specs=[VMEM, VMEM],
+        out_specs=VMEM,
+        compiler_params=PARAMS,
+        name="widen_own",
+    )(own_in, own_out)
+
+
+def add_kernel(grad_in, grad_out, received, total, other_in, other_out, sems):
+    half = 1 - lax.axis_index("dp")
     copy_in = pltpu.make_async_copy(
-        grad_in.at[:, pl.ds(pl.multiple_of(half * HALF_IN, 128), HALF_IN)], buf_in, sems.at[0]
+        grad_in.at[:, pl.ds(pl.multiple_of(half * HALF_IN, 128), HALF_IN)], other_in, sems.at[0]
     )
     copy_out = pltpu.make_async_copy(
-        grad_out.at[:, pl.ds(pl.multiple_of(half * HALF_OUT, 128), HALF_OUT)], buf_out, sems.at[1]
+        grad_out.at[:, pl.ds(pl.multiple_of(half * HALF_OUT, 128), HALF_OUT)], other_out, sems.at[1]
     )
     copy_in.start()
     copy_out.start()
     copy_in.wait()
-    packed[0:64, :] = buf_in[...].astype(F32)
+    total[0:64, :] = received[0:64, :] + other_in[...].astype(F32)
     copy_out.wait()
     for k in range(BLOCKS):
-        packed[64:128, pl.ds(k * HALF_OUT, HALF_OUT)] = buf_out[pl.ds(64 * k, 64), :].astype(F32)
-
-
-def widen(other, grad_in, grad_out):
-    return pl.pallas_call(
-        lambda *refs: widen_kernel(other, *refs),
+        block = pl.ds(k * HALF_OUT, HALF_OUT)
+        total[64:128, block] = received[64:128, block] + other_out[pl.ds(64 * k, 64), :].astype(F32)
+
+
+def add_other(grad_in, grad_out, received):
+    return pl.pallas_call(
+        add_kernel,
         out_shape=jax.ShapeDtypeStruct(PACK, F32),
-        in_specs=[HBM, HBM],
+        in_specs=[HBM, HBM, VMEM],
         out_specs=VMEM,
         scratch_shapes=[
             pltpu.VMEM((ROWS_IN, HALF_IN), jnp.bfloat16),
             pltpu.VMEM((ROWS_OUT, HALF_OUT), jnp.bfloat16),
             pltpu.SemaphoreType.DMA((2,)),
         ],
-        compiler_params=PARAMS,
-        name="widen_other" if other else "widen_own",
-    )(grad_in, grad_out)
+        input_output_aliases={2: 0},
+        cost_estimate=pl.CostEstimate(flops=262144, bytes_accessed=3 * 1024 * 1024, transcendentals=0),
+        compiler_params=pltpu.CompilerParams(vmem_limit_bytes=4 * 1024 * 1024),
+        name="add_other",
+    )(grad_in, grad_out, received)
 
 
 def rows_kernel(own, received, summed, row_sums):
@@ -194,11 +275,22 @@
 
 
 def update_kernel(
-    factors, scaled, row_scale, other, received, update_in, update_out, cols_in, cols_out, buf_in, buf_out, sems
+    factors, scaled, row_scale, other, rows_in_new, rows_out_new,
+    update_in, update_out, rows_in, rows_out, cols_in, cols_out,
+    buf_in, buf_out, buf_cols, sems,
 ):
     own_half = lax.axis_index("dp")
     my_x = lax.axis_index("x")
     lane = lax.broadcasted_iota(jnp.int32, (1, 128), 1)
+    copies = []
+
+    def write(source, target):
+        copy = pltpu.make_async_copy(source, target, sems.at[len(copies)])
+        copy.start()
+        copies.append(copy)
+
+    write(rows_in_new, rows_in)
+    write(rows_out_new, rows_out)
     energies = jnp.sum(factors[:, :, 256:384], axis=0)
 
     def limit(at):
@@ -215,87 +307,91 @@
         right = factors[(half * 8 + 2 * tile + 1) * 4 + my_x, :, lanes(2)]
         return jnp.where(lane < 64, left, pltpu.roll(right, 64, 1))
 
-    copies = []
-    for which in range(2):
-        half = own_half if which == 0 else 1 - own_half
+    def block(buffer, target, offset, width, start):
+        write(
+            buffer.at[:, pl.ds(start, width)],
+            target.at[:, pl.ds(pl.multiple_of(offset + start, 128), width)],
+        )
+
+    for which, half, source in ((0, own_half, scaled), (1, 1 - own_half, other)):
 
         def value(row, scale_row, tile):
-            if which == 0:
-                return scaled[pl.ds(row, 64), lanes(tile)]
-            both = other[pl.ds(row, 64), lanes(tile)] + received[pl.ds(row, 64), lanes(tile)]
-            return both * row_scale[pl.ds(scale_row, 64), :]
+            rows = source[pl.ds(row, 64), lanes(tile)]
+            return rows if which == 0 else rows * row_scale[pl.ds(scale_row, 64), :]
 
         for tile in range(TILES_IN):
             factor = factor_in(half, tile)
+            buf_cols[pl.ds(half * TILES_IN + tile, 1), :] = factor
             buf_in[which, :, lanes(tile)] = value(0, 0, tile) * (lax.rsqrt(factor) * limit_in)
-        copy = pltpu.make_async_copy(
-            buf_in.at[which],
-            update_in.at[:, pl.ds(pl.multiple_of(half * HALF_IN, 128), HALF_IN)],
-            sems.at[2 * which],
-        )
-        copy.start()
-        copies.append(copy)
+            if tile % 4 == 3:
+                block(buf_in.at[which], update_in, half * HALF_IN, 512, (tile - 3) * 128)
         for tile in range(TILES_OUT):
-            scale = lax.rsqrt(factor_out(half, tile)) * limit_out
+            factor = factor_out(half, tile)
+            buf_cols[pl.ds(32 + half * TILES_OUT + tile, 1), :] = factor
+            scale = lax.rsqrt(factor) * limit_out
             for k in range(BLOCKS):
                 buf_out[which, pl.ds(64 * k, 64), lanes(tile)] = (
                     value(64, 64 + 64 * k, k * TILES_OUT + tile) * scale
                 )
-        copy = pltpu.make_async_copy(
-            buf_out.at[which],
-            update_out.at[:, pl.ds(pl.multiple_of(half * HALF_OUT, 128), HALF_OUT)],
-            sems.at[2 * which + 1],
-        )
-        copy.start()
-        copies.append(copy)
-    for half in range(2):
-        for tile in range(TILES_IN):
-            cols_in[pl.ds(half * TILES_IN + tile, 1), :] = factor_in(half, tile)
-        for tile in range(TILES_OUT):
-            cols_out[pl.ds(half * TILES_OUT + tile, 1), :] = factor_out(half, tile)
+            if tile % 2 == 1:
+                block(buf_out.at[which], update_out, half * HALF_OUT, 256, (tile - 1) * 128)
+    write(buf_cols.at[0:32, :], cols_in)
+    write(buf_cols.at[32:40, :], cols_out)
     for copy in copies:
         copy.wait()
 
 
-def update_of(factors, scaled, row_scale, other, received):
+def update_of(factors, scaled, row_scale, other, rows_in_new, rows_out_new):
     return pl.pallas_call(
         update_kernel,
         out_shape=(
             jax.ShapeDtypeStruct((ROWS_IN, COLS_IN), F32),
             jax.ShapeDtypeStruct((ROWS_OUT, COLS_OUT), F32),
+            jax.ShapeDtypeStruct((1, ROWS_IN), F32),
+            jax.ShapeDtypeStruct((1, ROWS_OUT), F32),
             jax.ShapeDtypeStruct((COLS_IN // 128, 128), F32),
             jax.ShapeDtypeStruct((COLS_OUT // 128, 128), F32),
         ),
-        in_specs=[VMEM] * 5,
-        out_specs=(HBM, HBM, VMEM, VMEM),
+        in_specs=[VMEM] * 6,
+        out_specs=(HBM,) * 6,
         scratch_shapes=[
             pltpu.VMEM((2, ROWS_IN, HALF_IN), F32),
             pltpu.VMEM((2, ROWS_OUT, HALF_OUT), F32),
-            pltpu.SemaphoreType.DMA((4,)),
+            pltpu.VMEM((40, 128), F32),
+            pltpu.SemaphoreType.DMA((16,)),
         ],
         compiler_params=PARAMS,
         name="update",
-    )(factors, scaled, row_scale, other, received)
+    )(factors, scaled, row_scale, other, rows_in_new, rows_out_new)
+
+
+def keep_in_hbm(x):
+    return pltpu.with_memory_space_constraint(x, pltpu.HBM)
 
 
 def per_device(grad_in, grad_out, rows_in, cols_in, rows_out, cols_out):
-    grad_in, grad_out = grad_in[0], grad_out[0]
     swap = [(0, 1), (1, 0)]
-    other = widen(True, grad_in, grad_out)
-    arrived_own = lax.ppermute(other, "dp", swap)
-    own = widen(False, grad_in, grad_out)
+    grad_in, grad_out = keep_in_hbm(grad_in[0]), keep_in_hbm(grad_out[0])
+    first, own_in, own_out, rows_in, rows_out, cols_in, cols_out = fetch(
+        grad_in,
+        grad_out,
+        keep_in_hbm(rows_in.reshape(1, ROWS_IN)),
+        keep_in_hbm(rows_out.reshape(1, ROWS_OUT)),
+        keep_in_hbm(cols_in.reshape(16, 1, 256)),
+        keep_in_hbm(cols_out.reshape(8, 1, 128)),
+    )
+    arrived_own = lax.ppermute(first, "dp", swap)
+    own = widen_own(own_in, own_out)
     arrived_other = lax.ppermute(own, "dp", swap)
 
     summed, row_sums = row_sums_of(own, arrived_own)
     row_sums = lax.all_to_all(row_sums, ("dp", "x"), 0, 0)
-    scaled, row_scale, new_rows_in, new_rows_out, sums = column_sums_of(
-        row_sums, rows_in.reshape(1, ROWS_IN), rows_out.reshape(1, ROWS_OUT), summed
-    )
+    other = add_other(grad_in, grad_out, arrived_other)
+    scaled, row_scale, new_rows_in, new_rows_out, sums = column_sums_of(row_sums, rows_in, rows_out, summed)
     sums = lax.all_to_all(sums, ("z", "y"), 0, 0)
-    factors = factors_of(sums, cols_in.reshape(16, 1, 256), cols_out.reshape(8, 1, 128))
-    factors = lax.all_to_all(factors, ("dp", "z", "x"), 0, 0)
-    update_in, update_out, new_cols_in, new_cols_out = update_of(
-        factors, scaled, row_scale, other, arrived_other
+    factors = lax.all_to_all(factors_of(sums, cols_in, cols_out), ("dp", "z", "x"), 0, 0)
+    update_in, update_out, new_rows_in, new_rows_out, new_cols_in, new_cols_out = update_of(
+        factors, scaled, row_scale, other, new_rows_in, new_rows_out
     )
     return (
         update_in,

time: 70.2 us -> 65 us (0.926)
  local copies, waits for them, and re-layouts: 4.96 us -> 0 us
  waiting for transfers between devices: 10.3 us -> 9.15 us
  Pallas kernels: 4.46 us -> 5.6 us
    unnamed x16 -> x0, local copies, waits for them, and re-layouts: 4.96 us -> none
    pallas_call x2 -> x3, Pallas kernels: 0.27 us -> 2.52 us  [the longest x1 1.28 us: fetch(): pl.pallas_call(fetch_kernel, out_shape=(jax.ShapeDtypeStruct(PACK, F32),...]
    all_to_all x1, waiting for transfers between devices: 10.1 us -> 8.89 us  [per_device(): lax.all_to_all(factors_of(sums, cols_in, cols_out), ('dp', 'z', 'x'), 0, 0)]
  transfers between devices with their start and end apart: 3 -> 3, of which waited for: 2 -> 2; matrix products, arithmetic and copies ran while one was open for 0% -> 0% of each run, Pallas kernels for 3% -> 4%
where the time goes in v2:
time: 65 us; the launch traced here: 64.6 us
  blocking collectives  31.9 us (49%)
  starting transfers between devices  17.3 us (27%)
  waiting for transfers between devices  9.15 us (14%)
  Pallas kernels  5.6 us (9%)
  between operations  0.7 us (1%)
    all_to_all x1, blocking collectives, per_device(): sums = lax.all_to_all(sums, ('z', 'y'), 0, 0)  24.3 us
    all_to_all x1, waiting for transfers between devices, per_device(): lax.all_to_all(factors_of(sums, cols_in, cols_out), ('dp', 'z', 'x'), 0, 0)  8.89 us
    ppermute x1, starting transfers between devices, per_device(): arrived_own = lax.ppermute(first, 'dp', swap)  8.79 us
    all_to_all x1, blocking collectives, per_device(): row_sums = lax.all_to_all(row_sums, ('dp', 'x'), 0, 0)  7.62 us
    all_to_all x1, starting transfers between devices, per_device(): lax.all_to_all(factors_of(sums, cols_in, cols_out), ('dp', 'z', 'x'), 0, 0)  6.6 us
    ppermute x1, starting transfers between devices, per_device(): arrived_other = lax.ppermute(own, 'dp', swap)  1.92 us
    pallas_call x1, Pallas kernels, update_of(): pl.pallas_call(update_kernel, out_shape=(jax.ShapeDtypeStruct((ROWS_IN, C...  1.63 us
  transfers between devices with their start and end apart: 3, of which 2 were waited for; matrix products, arithmetic and copies ran while one was open for 0% of the time, Pallas kernels for 4%

profile of v2, /device:TPU:1, one launch (start us, length us, event | category | flops | bytes accessed | tf_op | source)
XLA Modules:
  0.0 64.6 jit_solution(15439681628140523446)
XLA Ops:
  0.6 1.3 %fetch.1 = (f32[128,2048]{1,0:T(8,128)S(1)}, bf16[64,2048]{1,0:T(8,128)(2,1)S(1)}, bf16[256,512]{1,0:T(8,128)(2,1)S(1)}, f32[1,64]{1,0:T(1,128)S(1)}, f32[1,256]...) custom-call(bf16[64,4096]{1,0:T(8,128)(2,1)} %bitcast.10, bf16[256,1024]{1,0:T(8,128)(2,1)} %bitcast.12, ...), custom_call_target="tpu_custom_call" | custom-call | tf_op jit(solution)/shard_map/fetch/pallas_call | solution.py:76
  1.9 8.8 %collective-permute-start = (f32[128,2048]{1,0:T(8,128)S(1)}, f32[128,2048]{1,0:T(8,128)S(1)}, u32[]{:S(2)}, u32[]{:S(2)}) collective-permute-start(f32[128,2048]{1,0:T(8,128)S(1)} %get-tuple-element.28), channel_id=1, source_target_pairs={{0,256},{256,0},{1,257},{257,1},{2,258},{258,2},{3,259},{259,3},{4... | collective-permute-start | bytes 3145736 | tf_op jit(solution)/shard_map/ppermute | solution.py:383
  10.7 0.1 widen_own.1.own
  10.8 1.9 %collective-permute-start.1 = (f32[128,2048]{1,0:T(8,128)S(1)}, f32[128,2048]{1,0:T(8,128)S(1)}, u32[]{:S(2)}, u32[]{:S(2)}) collective-permute-start(f32[128,2048]{1,0:T(8,128)S(1)} %widen_own.1.own), channel_id=1, source_target_pairs={{0,256},{256,0},{1,257},{257,1},{2,258},{258,2},{3,259},{259,3},{4... | collective-permute-start | bytes 3145736 | tf_op jit(solution)/shard_map/ppermute | solution.py:385
  12.7 0.3 collective-permute-done.received
  13.0 0.2 row_sums.1
  13.2 7.6 %all_to_all.15.row_sums = f32[8,1,384]{2,1,0:T(1,128)S(1)} all-to-all(f32[8,1,384]{2,1,0:T(1,128)S(1)} %get-tuple-element.29), channel_id=1, replica_groups=mesh['dp'=2,'z'=8,'y'=8,'x'=4] {'dp','x'}, dimensions={0} | all-to-all | bytes 24576 | tf_op jit(solution)/shard_map/all_to_all | solution.py:388
  20.8 0.3 column_sums.1
  21.2 24.3 %all_to_all.16.sums = f32[64,1,640]{2,1,0:T(1,128)S(1)} all-to-all(f32[64,1,640]{2,1,0:T(1,128)S(1)} %get-tuple-element.33), channel_id=1, replica_groups=mesh['dp'=2,'z'=8,'y'=8,'x'=4] {'z','y'}, dimensions={0} | all-to-all | bytes 327680 | tf_op jit(solution)/shard_map/all_to_all | solution.py:391
  45.4 0.9 %column_factors.1 = f32[64,1,384]{2,1,0:T(1,128)} custom-call(f32[64,1,640]{2,1,0:T(1,128)S(1)} %all_to_all.16.sums, f32[16,1,256]{2,1,0:T(1,128)S(1)} %get-tuple-element.34.cols_in, f32[8,1,128]{2,1,0:T(1,128)S(1)} %get-tuple-element.35.cols_out), custom_call_target="tpu_custom_call" | custom-call | tf_op jit(solution)/shard_map/column_factors/pallas_call | solution.py:267
  46.3 6.6 %all-to-all-start.2 = ((f32[64,1,384]{2,1,0:T(1,128)}), f32[64,1,384]{2,1,0:T(1,128)S(1)}, u32[]{:S(2)}, u32[]{:S(2)}) async-start(f32[64,1,384]{2,1,0:T(1,128)} %column_factors.1), calls=%async_computation.2 | async-start | bytes 196608 | tf_op jit(solution)/shard_map/all_to_all | solution.py:392
  52.9 0.0 collective-permute-done.1.received
  52.9 1.2 %add_other.1.other = f32[128,2048]{1,0:T(8,128)S(1)} custom-call(bf16[64,4096]{1,0:T(8,128)(2,1)} %bitcast.11, bf16[256,1024]{1,0:T(8,128)(2,1)} %bitcast.13, f32[128,2048]{1,0:T(8,128)S(1)} %collective-permute-done.1.received), custom_call_target="tpu_custom_call", output_to_operand_aliasing={{}: (2, {})} | custom-call | flops 262144 | bytes 3145728 | tf_op jit(solution)/shard_map/add_other/pallas_call | solution.py:131
  54.1 8.9 %all-to-all-done.2.factors = f32[64,1,384]{2,1,0:T(1,128)S(1)} async-done(((f32[64,1,384]{2,1,0:T(1,128)}), f32[64,1,384]{2,1,0:T(1,128)S(1)}, u32[]{:S(2)}, u32[]{:S(2)}) %all-to-all-start.2) | async-done | bytes 98336 | tf_op jit(solution)/shard_map/all_to_all | solution.py:392
  63.0 1.6 %update.1 = (f32[64,4096]{1,0:T(8,128)}, f32[256,1024]{1,0:T(8,128)}, f32[1,64]{1,0:T(1,128)}, f32[1,256]{1,0:T(1,128)}, f32[32,128]{1,0:T(8,128)}, /*index=5*/f32[8,128]{1,0:T(8,128)}) custom-call(f32[64,1,384]{2,1,0:T(1,128)S(1)} %all-to-all-done.2.factors, f32[128,2048]{1,0:T(8,128)S(1)} %get-tuple-element.36.scaled, ...), custom_call_target="tpu_custom_call" | custom-call | tf_op jit(solution)/shard_map/update/pallas_call | solution.py:345
Async XLA Ops:
  1.9 11.1 %collective-permute-start = (f32[128,2048]{1,0:T(8,128)S(1)}, f32[128,2048]{1,0:T(8,128)S(1)}, u32[]{:S(2)}, u32[]{:S(2)}) collective-permute-start(f32[128,2048]{1,0:T(8,128)S(1)} %get-tuple-element.28), channel_id=1, source_target_pairs={{0,256},{256,0},{1,257},{257,1},{2,258},{258,2},{3,259},{259,3},{4... | collective-permute-start | bytes 3145736 | tf_op jit(solution)/shard_map/ppermute | solution.py:383
  10.8 42.1 %collective-permute-start.1 = (f32[128,2048]{1,0:T(8,128)S(1)}, f32[128,2048]{1,0:T(8,128)S(1)}, u32[]{:S(2)}, u32[]{:S(2)}) collective-permute-start(f32[128,2048]{1,0:T(8,128)S(1)} %widen_own.1.own), channel_id=1, source_target_pairs={{0,256},{256,0},{1,257},{257,1},{2,258},{258,2},{3,259},{259,3},{4... | collective-permute-start | bytes 3145736 | tf_op jit(solution)/shard_map/ppermute | solution.py:385
  46.3 16.7 %all-to-all-start.2 = ((f32[64,1,384]{2,1,0:T(1,128)}), f32[64,1,384]{2,1,0:T(1,128)S(1)}, u32[]{:S(2)}, u32[]{:S(2)}) async-start(f32[64,1,384]{2,1,0:T(1,128)} %column_factors.1), calls=%async_computation.2 | async-start | bytes 196608 | tf_op jit(solution)/shard_map/all_to_all | solution.py:392

commit v3 on v2

--- a/solution.py
+++ b/solution.py
@@ -22,6 +22,7 @@
 F32 = jnp.float32
 VMEM = pl.BlockSpec(memory_space=pltpu.VMEM)
 HBM = pl.BlockSpec(memory_space=pltpu.HBM)
+ANY = pl.BlockSpec(memory_space=pl.ANY)
 PARAMS = pltpu.CompilerParams(vmem_limit_bytes=16 * 1024 * 1024)
 
 
@@ -181,7 +182,10 @@
     )(own, received)
 
 
-def columns_kernel(row_sums, rows_in, rows_out, summed, scaled, row_scale, new_in, new_out, sends):
+def columns_kernel(
+    row_sums, rows_in, rows_out, summed, other, scaled, row_scale, new_in, new_out, sends, other_on
+):
+    del other, other_on
     total = jnp.sum(row_sums[...], axis=0)
     fresh_in = DECAY * rows_in[...] + (1.0 - DECAY) * (total[:, 0:64] * (1.0 / FF) + EPSILON)
     fresh_out = DECAY * rows_out[...] + (1.0 - DECAY) * (total[:, 128:384] * (1.0 / D) + EPSILON)
@@ -209,26 +213,26 @@
     def fold(value):
         return jnp.sum(value, axis=0, keepdims=True)
 
-    def send(chunk, at, vector):
-        for peer in range(8):
-            sends[chunk * 8 + peer, :, lanes(at)] = vector
+    def send(chunk, row, vector):
+        for peer in range(chunk, 8, 2):
+            sends[peer, pl.ds(row, 1), :] = vector
 
     for tile in range(TILES_IN):
         plain, weighted = column(0, 0, tile)
-        send(tile // 2, tile % 2, fold(plain))
-        send(tile // 2, 2 + tile % 2, fold(weighted))
-    lane = lax.broadcasted_iota(jnp.int32, (1, 128), 1)
+        send(tile // 8, tile % 8, fold(plain))
+        send(tile // 8, 8 + tile % 8, fold(weighted))
     for tile in range(TILES_OUT):
         plain, weighted = column(64, 64, tile)
         for k in range(1, BLOCKS):
             more = column(64, 64 + 64 * k, k * TILES_OUT + tile)
             plain, weighted = plain + more[0], weighted + more[1]
-        plain, weighted = fold(plain), fold(weighted)
-        send(2 * tile, 4, jnp.where(lane < 64, plain, pltpu.roll(weighted, 64, 1)))
-        send(2 * tile + 1, 4, jnp.where(lane < 64, pltpu.roll(plain, 64, 1), weighted))
-
-
-def column_sums_of(row_sums, rows_in, rows_out, summed):
+        send(tile // 2, 16 + tile % 2, fold(plain))
+        send(tile // 2, 18 + tile % 2, fold(weighted))
+    for peer in range(8):
+        sends[peer, 20:24, :] = jnp.zeros((4, 128), F32)
+
+
+def column_sums_of(row_sums, rows_in, rows_out, summed, other):
     return pl.pallas_call(
         columns_kernel,
         out_shape=(
@@ -236,37 +240,57 @@
             jax.ShapeDtypeStruct((320, 128), F32),
             jax.ShapeDtypeStruct((1, ROWS_IN), F32),
             jax.ShapeDtypeStruct((1, ROWS_OUT), F32),
-            jax.ShapeDtypeStruct((64, 1, 640), F32),
+            jax.ShapeDtypeStruct((8, 24, 128), F32),
+            jax.ShapeDtypeStruct(PACK, F32),
         ),
-        in_specs=[VMEM] * 4,
-        out_specs=(VMEM,) * 5,
+        in_specs=[VMEM] * 4 + [ANY],
+        out_specs=(VMEM,) * 5 + (ANY,),
+        input_output_aliases={4: 5},
         compiler_params=PARAMS,
         name="column_sums",
-    )(row_sums, rows_in, rows_out, summed)
+    )(row_sums, rows_in, rows_out, summed, other)
+
+
+def total_kernel(sums, sends):
+    total = sums[0]
+    for peer in range(1, 8):
+        total = total + sums[peer]
+    for peer in range(8):
+        sends[peer] = total
+
+
+def total_of(sums):
+    return pl.pallas_call(
+        total_kernel,
+        out_shape=jax.ShapeDtypeStruct((8, 24, 128), F32),
+        in_specs=[VMEM],
+        out_specs=VMEM,
+        compiler_params=PARAMS,
+        name="total",
+    )(sums)
 
 
 def factors_kernel(sums, cols_in, cols_out, sends):
-    owner = lax.axis_index("dp") * 8 + lax.axis_index("z")
-    total = jnp.sum(sums[...], axis=0)
-    lane = lax.broadcasted_iota(jnp.int32, (1, 128), 1)
-    new_in = DECAY * cols_in[owner] + (1.0 - DECAY) * (total[:, 0:256] * (1.0 / D) + EPSILON)
-    energy_in = jnp.sum(total[:, 256:512] / new_in, axis=1, keepdims=True)
-    mixed = total[:, 512:640]
-    old_out = cols_out[owner // 2]
-    old_out = jnp.where(owner % 2 == 1, pltpu.roll(old_out, 64, 1), old_out)
-    new_out = DECAY * old_out + (1.0 - DECAY) * (mixed * (1.0 / FF) + EPSILON)
-    weighted = jnp.where(lane < 64, pltpu.roll(mixed, 64, 1) / new_out, 0.0)
-    energy_out = jnp.sum(weighted, axis=1, keepdims=True)
-    last = jnp.where(lane < 64, new_out, jnp.where(lane < 96, energy_in, energy_out))
-    for peer in range(64):
-        sends[peer, :, 0:256] = new_in
-        sends[peer, :, 256:384] = last
+    chunk = lax.axis_index("dp") * 2 + lax.axis_index("pair")
+    total = sums[0]
+    for peer in range(1, 8):
+        total = total + sums[peer]
+    new_in = DECAY * cols_in[chunk] + (1.0 - DECAY) * (total[0:8] * (1.0 / D) + EPSILON)
+    new_out = DECAY * cols_out[chunk] + (1.0 - DECAY) * (total[16:18] * (1.0 / FF) + EPSILON)
+    energy_in = jnp.sum(total[8:16] / new_in, axis=0, keepdims=True)
+    energy_out = jnp.sum(total[18:20] / new_out, axis=0, keepdims=True)
+    for peer in range(16):
+        sends[peer, 0:8, :] = new_in
+        sends[peer, 8:10, :] = new_out
+        sends[peer, 10:11, :] = energy_in
+        sends[peer, 11:12, :] = energy_out
+        sends[peer, 12:16, :] = jnp.zeros((4, 128), F32)
 
 
 def factors_of(sums, cols_in, cols_out):
     return pl.pallas_call(
         factors_kernel,
-        out_shape=jax.ShapeDtypeStruct((64, 1, 384), F32),
+        out_shape=jax.ShapeDtypeStruct((16, 16, 128), F32),
         in_specs=[VMEM] * 3,
         out_specs=VMEM,
         compiler_params=PARAMS,
@@ -281,7 +305,6 @@
 ):
     own_half = lax.axis_index("dp")
     my_x = lax.axis_index("x")
-    lane = lax.broadcasted_iota(jnp.int32, (1, 128), 1)
     copies = []
 
     def write(source, target):
@@ -291,21 +314,21 @@
 
     write(rows_in_new, rows_in)
     write(rows_out_new, rows_out)
-    energies = jnp.sum(factors[:, :, 256:384], axis=0)
-
-    def limit(at):
-        energy = jnp.sum(jnp.where(lane == at, energies, 0.0), axis=1, keepdims=True)
+
+    def limit(row):
+        parts = factors[0, row : row + 1, :]
+        for peer in range(1, 16):
+            parts = parts + factors[peer, row : row + 1, :]
+        energy = jnp.sum(parts, axis=1, keepdims=True)
         return 1.0 / jnp.maximum(1.0, jnp.sqrt(energy * (1.0 / (D * FF))))
 
-    limit_in, limit_out = limit(64), limit(96)
+    limit_in, limit_out = limit(10), limit(11)
 
     def factor_in(half, tile):
-        return factors[(half * 8 + tile // 2) * 4 + my_x, :, lanes(tile % 2)]
+        return factors[(half * 2 + tile // 8) * 4 + my_x, pl.ds(tile % 8, 1), :]
 
     def factor_out(half, tile):
-        left = factors[(half * 8 + 2 * tile) * 4 + my_x, :, lanes(2)]
-        right = factors[(half * 8 + 2 * tile + 1) * 4 + my_x, :, lanes(2)]
-        return jnp.where(lane < 64, left, pltpu.roll(right, 64, 1))
+        return factors[(half * 2 + tile // 2) * 4 + my_x, pl.ds(8 + tile % 2, 1), :]
 
     def block(buffer, target, offset, width, start):
         write(
@@ -377,8 +400,8 @@
         grad_out,
         keep_in_hbm(rows_in.reshape(1, ROWS_IN)),
         keep_in_hbm(rows_out.reshape(1, ROWS_OUT)),
-        keep_in_hbm(cols_in.reshape(16, 1, 256)),
-        keep_in_hbm(cols_out.reshape(8, 1, 128)),
+        keep_in_hbm(cols_in.reshape(4, 8, 128)),
+        keep_in_hbm(cols_out.reshape(4, 2, 128)),
     )
     arrived_own = lax.ppermute(first, "dp", swap)
     own = widen_own(own_in, own_out)
@@ -387,9 +410,12 @@
     summed, row_sums = row_sums_of(own, arrived_own)
     row_sums = lax.all_to_all(row_sums, ("dp", "x"), 0, 0)
     other = add_other(grad_in, grad_out, arrived_other)
-    scaled, row_scale, new_rows_in, new_rows_out, sums = column_sums_of(row_sums, rows_in, rows_out, summed)
-    sums = lax.all_to_all(sums, ("z", "y"), 0, 0)
-    factors = lax.all_to_all(factors_of(sums, cols_in, cols_out), ("dp", "z", "x"), 0, 0)
+    scaled, row_scale, new_rows_in, new_rows_out, sums, other = column_sums_of(
+        row_sums, rows_in, rows_out, summed, other
+    )
+    sums = lax.all_to_all(sums, ("y", "pair"), 0, 0)
+    sums = lax.all_to_all(total_of(sums), "z", 0, 0)
+    factors = lax.all_to_all(factors_of(sums, cols_in, cols_out), ("dp", "pair", "x"), 0, 0)
     update_in, update_out, new_rows_in, new_rows_out, new_cols_in, new_cols_out = update_of(
         factors, scaled, row_scale, other, new_rows_in, new_rows_out
     )
@@ -404,8 +430,8 @@
 
 
 def solution(mesh):
-    fine = Mesh(mesh.devices.reshape(2, 8, 8, 4), ("dp", "z", "y", "x"))
-    row = ("z", "y")
+    fine = Mesh(mesh.devices.reshape(2, 8, 4, 2, 4), ("dp", "z", "y", "pair", "x"))
+    row = ("z", "y", "pair")
     return jax.shard_map(
         per_device,
         mesh=fine,

time: 65 us -> 64 us (0.985)
  blocking collectives: 31.9 us -> 39.4 us
  waiting for transfers between devices: 9.15 us -> 3.97 us
  starting transfers between devices: 17.3 us -> 14.3 us
    all_to_all x2 -> x3, blocking collectives: 31.9 us -> 39.4 us  [the longest x1 17.3 us: per_device(): sums = lax.all_to_all(total_of(sums), 'z', 0, 0)]
    all_to_all x1, waiting for transfers between devices: 8.89 us -> 3.71 us  [per_device(): row_sums = lax.all_to_all(row_sums, ('dp', 'x'), 0, 0)]
    all_to_all x1, starting transfers between devices: 6.6 us -> 3.63 us  [per_device(): row_sums = lax.all_to_all(row_sums, ('dp', 'x'), 0, 0)]
    pallas_call x1 -> x2, Pallas kernels: 0.89 us -> 0.05 us  [the longest x1 0.04 us: factors_of(): pl.pallas_call(factors_kernel, out_shape=jax.ShapeDtypeStruct((16, 16, 12...]
  transfers between devices with their start and end apart: 3 -> 3, of which waited for: 2 -> 2; matrix products, arithmetic and copies ran while one was open for 0% -> 0% of each run, Pallas kernels for 4% -> 3%
where the time goes in v3:
time: 64 us; the launch traced here: 63.6 us
  blocking collectives  39.4 us (62%)
  starting transfers between devices  14.3 us (22%)
  Pallas kernels  5.22 us (8%)
  waiting for transfers between devices  3.97 us (6%)
  between operations  0.69 us (1%)
    all_to_all x1, blocking collectives, per_device(): sums = lax.all_to_all(total_of(sums), 'z', 0, 0)  17.3 us
    all_to_all x1, blocking collectives, per_device(): lax.all_to_all(factors_of(sums, cols_in, cols_out), ('dp', 'pair', 'x'),...  12.2 us
    all_to_all x1, blocking collectives, per_device(): sums = lax.all_to_all(sums, ('y', 'pair'), 0, 0)  9.83 us
    ppermute x1, starting transfers between devices, per_device(): arrived_own = lax.ppermute(first, 'dp', swap)  8.79 us
    all_to_all x1, waiting for transfers between devices, per_device(): row_sums = lax.all_to_all(row_sums, ('dp', 'x'), 0, 0)  3.71 us
    all_to_all x1, starting transfers between devices, per_device(): row_sums = lax.all_to_all(row_sums, ('dp', 'x'), 0, 0)  3.63 us
    ppermute x1, starting transfers between devices, per_device(): arrived_other = lax.ppermute(own, 'dp', swap)  1.92 us
    pallas_call x1, Pallas kernels, update_of(): pl.pallas_call(update_kernel, out_shape=(jax.ShapeDtypeStruct((ROWS_IN, C...  1.57 us
  transfers between devices with their start and end apart: 3, of which 2 were waited for; matrix products, arithmetic and copies ran while one was open for 0% of the time, Pallas kernels for 3%

profile of v3, /device:TPU:1, one launch (start us, length us, event | category | flops | bytes accessed | tf_op | source)
XLA Modules:
  0.0 63.6 jit_solution(5690477351425421297)
XLA Ops:
  0.6 1.3 %fetch.1 = (f32[128,2048]{1,0:T(8,128)S(1)}, bf16[64,2048]{1,0:T(8,128)(2,1)S(1)}, bf16[256,512]{1,0:T(8,128)(2,1)S(1)}, f32[1,64]{1,0:T(1,128)S(1)}, f32[1,256]...) custom-call(bf16[64,4096]{1,0:T(8,128)(2,1)} %bitcast.10, bf16[256,1024]{1,0:T(8,128)(2,1)} %bitcast.12, ...), custom_call_target="tpu_custom_call" | custom-call | tf_op jit(solution)/shard_map/fetch/pallas_call | solution.py:77
  1.9 8.8 %collective-permute-start = (f32[128,2048]{1,0:T(8,128)S(1)}, f32[128,2048]{1,0:T(8,128)S(1)}, u32[]{:S(2)}, u32[]{:S(2)}) collective-permute-start(f32[128,2048]{1,0:T(8,128)S(1)} %get-tuple-element.29), channel_id=1, source_target_pairs={{0,256},{256,0},{1,257},{257,1},{2,258},{258,2},{3,259},{259,3},{4... | collective-permute-start | bytes 3145736 | tf_op jit(solution)/shard_map/ppermute | solution.py:406
  10.7 0.1 widen_own.1.own
  10.8 1.9 %collective-permute-start.1 = (f32[128,2048]{1,0:T(8,128)S(1)}, f32[128,2048]{1,0:T(8,128)S(1)}, u32[]{:S(2)}, u32[]{:S(2)}) collective-permute-start(f32[128,2048]{1,0:T(8,128)S(1)} %widen_own.1.own), channel_id=1, source_target_pairs={{0,256},{256,0},{1,257},{257,1},{2,258},{258,2},{3,259},{259,3},{4... | collective-permute-start | bytes 3145736 | tf_op jit(solution)/shard_map/ppermute | solution.py:408
  12.7 0.3 collective-permute-done.received
  13.0 0.8 %row_sums.1 = (f32[128,2048]{1,0:T(8,128)S(1)}, f32[8,1,384]{2,1,0:T(1,128)}) custom-call(f32[128,2048]{1,0:T(8,128)S(1)} %widen_own.1.own, f32[128,2048]{1,0:T(8,128)S(1)} %collective-permute-done.received), custom_call_target="tpu_custom_call" | custom-call | tf_op jit(solution)/shard_map/row_sums/pallas_call | solution.py:175
  13.8 3.6 %all-to-all-start = ((f32[8,1,384]{2,1,0:T(1,128)}), f32[8,1,384]{2,1,0:T(1,128)S(1)}, u32[]{:S(2)}, u32[]{:S(2)}) async-start(f32[8,1,384]{2,1,0:T(1,128)} %get-tuple-element.30), calls=%async_computation | async-start | bytes 24576 | tf_op jit(solution)/shard_map/all_to_all | solution.py:411
  17.4 0.0 collective-permute-done.1.received
  17.4 1.2 %add_other.1.other = f32[128,2048]{1,0:T(8,128)S(1)} custom-call(bf16[64,4096]{1,0:T(8,128)(2,1)} %bitcast.11, bf16[256,1024]{1,0:T(8,128)(2,1)} %bitcast.13, f32[128,2048]{1,0:T(8,128)S(1)} %collective-permute-done.1.received), custom_call_target="tpu_custom_call", output_to_operand_aliasing={{}: (2, {})} | custom-call | flops 262144 | bytes 3145728 | tf_op jit(solution)/shard_map/add_other/pallas_call | solution.py:132
  18.6 3.7 %all-to-all-done.row_sums = f32[8,1,384]{2,1,0:T(1,128)S(1)} async-done(((f32[8,1,384]{2,1,0:T(1,128)}), f32[8,1,384]{2,1,0:T(1,128)S(1)}, u32[]{:S(2)}, u32[]{:S(2)}) %all-to-all-start) | async-done | bytes 12320 | tf_op jit(solution)/shard_map/all_to_all | solution.py:411
  22.3 0.3 column_sums.1
  22.6 9.8 %all_to_all.20.sums = f32[8,24,128]{2,1,0:T(8,128)S(1)} all-to-all(f32[8,24,128]{2,1,0:T(8,128)S(1)} %get-tuple-element.34), channel_id=1, replica_groups=mesh['dp'=2,'z'=8,'y'=4,'pair'=2,'x'=4] {'y','pair'}, dimensions={0} | all-to-all | bytes 196608 | tf_op jit(solution)/shard_map/all_to_all | solution.py:416
  32.4 17.3 %all_to_all.21.sums = f32[8,24,128]{2,1,0:T(8,128)S(1)} all-to-all(f32[8,24,128]{2,1,0:T(8,128)S(1)} %total.1), channel_id=1, replica_groups=mesh['dp'=2,'z'=8,'y'=4,'pair'=2,'x'=4] {'z'}, dimensions={0} | all-to-all | bytes 196608 | tf_op jit(solution)/shard_map/all_to_all | solution.py:417
  49.8 12.2 %all_to_all.22.factors = f32[16,16,128]{2,1,0:T(8,128)S(1)} all-to-all(f32[16,16,128]{2,1,0:T(8,128)S(1)} %column_factors.1), channel_id=1, replica_groups=mesh['dp'=2,'z'=8,'y'=4,'pair'=2,'x'=4] {'dp','pair','x'}, dimensions={0} | all-to-all | bytes 262144 | tf_op jit(solution)/shard_map/all_to_all | solution.py:418
  62.0 1.6 %update.1 = (f32[64,4096]{1,0:T(8,128)}, f32[256,1024]{1,0:T(8,128)}, f32[1,64]{1,0:T(1,128)}, f32[1,256]{1,0:T(1,128)}, f32[32,128]{1,0:T(8,128)}, /*index=5*/f32[8,128]{1,0:T(8,128)}) custom-call(f32[16,16,128]{2,1,0:T(8,128)S(1)} %all_to_all.22.factors, f32[128,2048]{1,0:T(8,128)S(1)} %get-tuple-element.37.scaled, ...), custom_call_target="tpu_custom_call" | custom-call | tf_op jit(solution)/shard_map/update/pallas_call | solution.py:368
  (2 shorter events, 0.1 us)
Async XLA Ops:
  1.9 11.1 %collective-permute-start = (f32[128,2048]{1,0:T(8,128)S(1)}, f32[128,2048]{1,0:T(8,128)S(1)}, u32[]{:S(2)}, u32[]{:S(2)}) collective-permute-start(f32[128,2048]{1,0:T(8,128)S(1)} %get-tuple-element.29), channel_id=1, source_target_pairs={{0,256},{256,0},{1,257},{257,1},{2,258},{258,2},{3,259},{259,3},{4... | collective-permute-start | bytes 3145736 | tf_op jit(solution)/shard_map/ppermute | solution.py:406
  10.8 6.6 %collective-permute-start.1 = (f32[128,2048]{1,0:T(8,128)S(1)}, f32[128,2048]{1,0:T(8,128)S(1)}, u32[]{:S(2)}, u32[]{:S(2)}) collective-permute-start(f32[128,2048]{1,0:T(8,128)S(1)} %widen_own.1.own), channel_id=1, source_target_pairs={{0,256},{256,0},{1,257},{257,1},{2,258},{258,2},{3,259},{259,3},{4... | collective-permute-start | bytes 3145736 | tf_op jit(solution)/shard_map/ppermute | solution.py:408
  13.8 8.5 %all-to-all-start = ((f32[8,1,384]{2,1,0:T(1,128)}), f32[8,1,384]{2,1,0:T(1,128)S(1)}, u32[]{:S(2)}, u32[]{:S(2)}) async-start(f32[8,1,384]{2,1,0:T(1,128)} %get-tuple-element.30), calls=%async_computation | async-start | bytes 24576 | tf_op jit(solution)/shard_map/all_to_all | solution.py:411

commit v4 on v3

--- a/solution.py
+++ b/solution.py
@@ -30,76 +30,53 @@
     return pl.ds(tile * 128, 128)
 
 
-def widen_in(packed, block):
-    packed[0:64, :] = block[...].astype(F32)
-
-
-def widen_out(packed, block):
-    for k in range(BLOCKS):
-        packed[64:128, pl.ds(k * HALF_OUT, HALF_OUT)] = block[pl.ds(64 * k, 64), :].astype(F32)
-
-
-def fetch_kernel(
-    grad_in, grad_out, rows_in, rows_out, cols_in, cols_out,
-    other, own_in, own_out, rows_in_here, rows_out_here, cols_in_here, cols_out_here,
-    other_in, other_out, sems,
-):
-    own_half = lax.axis_index("dp")
-
-    def block_in(half):
-        return grad_in.at[:, pl.ds(pl.multiple_of(half * HALF_IN, 128), HALF_IN)]
-
-    def block_out(half):
-        return grad_out.at[:, pl.ds(pl.multiple_of(half * HALF_OUT, 128), HALF_OUT)]
-
-    pairs = (
-        (block_in(1 - own_half), other_in),
-        (block_out(1 - own_half), other_out),
-        (block_in(own_half), own_in),
-        (block_out(own_half), own_out),
-        (rows_in, rows_in_here),
-        (rows_out, rows_out_here),
-        (cols_in, cols_in_here),
-        (cols_out, cols_out_here),
-    )
-    copies = [pltpu.make_async_copy(src, dst, sems.at[at]) for at, (src, dst) in enumerate(pairs)]
+def half_copies(grad_in, grad_out, half, block_in, block_out, sems):
+    columns_in = pl.ds(pl.multiple_of(half * HALF_IN, 128), HALF_IN)
+    columns_out = pl.ds(pl.multiple_of(half * HALF_OUT, 128), HALF_OUT)
+    return (
+        pltpu.make_async_copy(grad_in.at[:, columns_in], block_in, sems.at[0]),
+        pltpu.make_async_copy(grad_out.at[:, columns_out], block_out, sems.at[1]),
+    )
+
+
+HALF_SCRATCH = [
+    pltpu.VMEM((ROWS_IN, HALF_IN), jnp.bfloat16),
+    pltpu.VMEM((ROWS_OUT, HALF_OUT), jnp.bfloat16),
+]
+
+
+def fetch_kernel(grad_in, grad_out, other, other_in, other_out, sems):
+    copies = half_copies(grad_in, grad_out, 1 - lax.axis_index("dp"), other_in, other_out, sems)
     for copy in copies:
         copy.start()
     copies[0].wait()
-    widen_in(other, other_in)
+    other[0:64, :] = other_in[...].astype(F32)
     copies[1].wait()
-    widen_out(other, other_out)
-    for copy in copies[2:]:
-        copy.wait()
-
-
-def fetch(grad_in, grad_out, rows_in, rows_out, cols_in, cols_out):
+    for k in range(BLOCKS):
+        other[64:128, pl.ds(k * HALF_OUT, HALF_OUT)] = other_out[pl.ds(64 * k, 64), :].astype(F32)
+
+
+def fetch(grad_in, grad_out):
     return pl.pallas_call(
         fetch_kernel,
-        out_shape=(
-            jax.ShapeDtypeStruct(PACK, F32),
-            jax.ShapeDtypeStruct((ROWS_IN, HALF_IN), jnp.bfloat16),
-            jax.ShapeDtypeStruct((ROWS_OUT, HALF_OUT), jnp.bfloat16),
-        )
-        + tuple(jax.ShapeDtypeStruct(x.shape, F32) for x in (rows_in, rows_out, cols_in, cols_out)),
-        in_specs=[HBM] * 6,
-        out_specs=(VMEM,) * 7,
-        scratch_shapes=[
-            pltpu.VMEM((ROWS_IN, HALF_IN), jnp.bfloat16),
-            pltpu.VMEM((ROWS_OUT, HALF_OUT), jnp.bfloat16),
-            pltpu.SemaphoreType.DMA((8,)),
-        ],
+        out_shape=jax.ShapeDtypeStruct(PACK, F32),
+        in_specs=[HBM, HBM],
+        out_specs=VMEM,
+        scratch_shapes=HALF_SCRATCH + [pltpu.SemaphoreType.DMA((2,))],
         compiler_params=PARAMS,
         name="fetch",
-    )(grad_in, grad_out, rows_in, rows_out, cols_in, cols_out)
-
-
-def widen_kernel(own_in, own_out, packed):
-    widen_in(packed, own_in)
-    widen_out(packed, own_out)
-
-
-def widen_own(own_in, own_out):
+    )(grad_in, grad_out)
+
+
+def widen_kernel(grad_in, grad_out, packed):
+    half = lax.axis_index("dp")
+    packed[0:64, :] = grad_in[:, pl.ds(pl.multiple_of(half * HALF_IN, 128), HALF_IN)].astype(F32)
+    columns = pl.ds(pl.multiple_of(half * HALF_OUT, 128), HALF_OUT)
+    for k in range(BLOCKS):
+        packed[64:128, pl.ds(k * HALF_OUT, HALF_OUT)] = grad_out[pl.ds(64 * k, 64), columns].astype(F32)
+
+
+def widen_own(grad_in, grad_out):
     return pl.pallas_call(
         widen_kernel,
         out_shape=jax.ShapeDtypeStruct(PACK, F32),
@@ -107,43 +84,37 @@
         out_specs=VMEM,
         compiler_params=PARAMS,
         name="widen_own",
-    )(own_in, own_out)
-
-
-def add_kernel(grad_in, grad_out, received, total, other_in, other_out, sems):
-    half = 1 - lax.axis_index("dp")
-    copy_in = pltpu.make_async_copy(
-        grad_in.at[:, pl.ds(pl.multiple_of(half * HALF_IN, 128), HALF_IN)], other_in, sems.at[0]
-    )
-    copy_out = pltpu.make_async_copy(
-        grad_out.at[:, pl.ds(pl.multiple_of(half * HALF_OUT, 128), HALF_OUT)], other_out, sems.at[1]
-    )
-    copy_in.start()
-    copy_out.start()
-    copy_in.wait()
+    )(grad_in, grad_out)
+
+
+def add_kernel(grad_in, grad_out, received, *refs):
+    total, other_in, other_out, sems = refs[4], refs[9], refs[10], refs[11]
+    copies = half_copies(grad_in, grad_out, 1 - lax.axis_index("dp"), other_in, other_out, sems)
+    small = [pltpu.make_async_copy(refs[at], refs[5 + at], sems.at[2 + at]) for at in range(4)]
+    for copy in (*copies, *small):
+        copy.start()
+    copies[0].wait()
     total[0:64, :] = received[0:64, :] + other_in[...].astype(F32)
-    copy_out.wait()
+    copies[1].wait()
     for k in range(BLOCKS):
         block = pl.ds(k * HALF_OUT, HALF_OUT)
         total[64:128, block] = received[64:128, block] + other_out[pl.ds(64 * k, 64), :].astype(F32)
-
-
-def add_other(grad_in, grad_out, received):
+    for copy in small:
+        copy.wait()
+
+
+def add_other(grad_in, grad_out, received, *factors):
     return pl.pallas_call(
         add_kernel,
-        out_shape=jax.ShapeDtypeStruct(PACK, F32),
-        in_specs=[HBM, HBM, VMEM],
-        out_specs=VMEM,
-        scratch_shapes=[
-            pltpu.VMEM((ROWS_IN, HALF_IN), jnp.bfloat16),
-            pltpu.VMEM((ROWS_OUT, HALF_OUT), jnp.bfloat16),
-            pltpu.SemaphoreType.DMA((2,)),
-        ],
+        out_shape=tuple(jax.ShapeDtypeStruct(x.shape, F32) for x in (received, *factors)),
+        in_specs=[HBM, HBM, VMEM] + [HBM] * 4,
+        out_specs=(VMEM,) * 5,
+        scratch_shapes=HALF_SCRATCH + [pltpu.SemaphoreType.DMA((6,))],
         input_output_aliases={2: 0},
         cost_estimate=pl.CostEstimate(flops=262144, bytes_accessed=3 * 1024 * 1024, transcendentals=0),
         compiler_params=pltpu.CompilerParams(vmem_limit_bytes=4 * 1024 * 1024),
         name="add_other",
-    )(grad_in, grad_out, received)
+    )(grad_in, grad_out, received, *factors)
 
 
 def rows_kernel(own, received, summed, row_sums):
@@ -215,7 +186,7 @@
 
     def send(chunk, row, vector):
         for peer in range(chunk, 8, 2):
-            sends[peer, pl.ds(row, 1), :] = vector
+            sends[peer, row // 4, row % 4 : row % 4 + 1, :] = vector
 
     for tile in range(TILES_IN):
         plain, weighted = column(0, 0, tile)
@@ -228,8 +199,6 @@
             plain, weighted = plain + more[0], weighted + more[1]
         send(tile // 2, 16 + tile % 2, fold(plain))
         send(tile // 2, 18 + tile % 2, fold(weighted))
-    for peer in range(8):
-        sends[peer, 20:24, :] = jnp.zeros((4, 128), F32)
 
 
 def column_sums_of(row_sums, rows_in, rows_out, summed, other):
@@ -240,7 +209,7 @@
             jax.ShapeDtypeStruct((320, 128), F32),
             jax.ShapeDtypeStruct((1, ROWS_IN), F32),
             jax.ShapeDtypeStruct((1, ROWS_OUT), F32),
-            jax.ShapeDtypeStruct((8, 24, 128), F32),
+            jax.ShapeDtypeStruct((8, 5, 4, 128), F32),
             jax.ShapeDtypeStruct(PACK, F32),
         ),
         in_specs=[VMEM] * 4 + [ANY],
@@ -262,7 +231,7 @@
 def total_of(sums):
     return pl.pallas_call(
         total_kernel,
-        out_shape=jax.ShapeDtypeStruct((8, 24, 128), F32),
+        out_shape=jax.ShapeDtypeStruct((8, 5, 4, 128), F32),
         in_specs=[VMEM],
         out_specs=VMEM,
         compiler_params=PARAMS,
@@ -275,22 +244,23 @@
     total = sums[0]
     for peer in range(1, 8):
         total = total + sums[peer]
-    new_in = DECAY * cols_in[chunk] + (1.0 - DECAY) * (total[0:8] * (1.0 / D) + EPSILON)
-    new_out = DECAY * cols_out[chunk] + (1.0 - DECAY) * (total[16:18] * (1.0 / FF) + EPSILON)
-    energy_in = jnp.sum(total[8:16] / new_in, axis=0, keepdims=True)
-    energy_out = jnp.sum(total[18:20] / new_out, axis=0, keepdims=True)
+    energy_in = jnp.zeros((1, 128), F32)
+    for part in range(2):
+        new_in = DECAY * cols_in[chunk * 2 + part] + (1.0 - DECAY) * (total[part] * (1.0 / D) + EPSILON)
+        energy_in += jnp.sum(total[2 + part] / new_in, axis=0, keepdims=True)
+        for peer in range(16):
+            sends[peer, part] = new_in
+    new_out = DECAY * cols_out[chunk] + (1.0 - DECAY) * (total[4, 0:2] * (1.0 / FF) + EPSILON)
+    energy_out = jnp.sum(total[4, 2:4] / new_out, axis=0, keepdims=True)
+    last = jnp.concatenate([new_out, energy_in, energy_out], axis=0)
     for peer in range(16):
-        sends[peer, 0:8, :] = new_in
-        sends[peer, 8:10, :] = new_out
-        sends[peer, 10:11, :] = energy_in
-        sends[peer, 11:12, :] = energy_out
-        sends[peer, 12:16, :] = jnp.zeros((4, 128), F32)
+        sends[peer, 2] = last
 
 
 def factors_of(sums, cols_in, cols_out):
     return pl.pallas_call(
         factors_kernel,
-        out_shape=jax.ShapeDtypeStruct((16, 16, 128), F32),
+        out_shape=jax.ShapeDtypeStruct((16, 3, 4, 128), F32),
         in_specs=[VMEM] * 3,
         out_specs=VMEM,
         compiler_params=PARAMS,
@@ -312,23 +282,22 @@
         copy.start()
         copies.append(copy)
 
-    write(rows_in_new, rows_in)
-    write(rows_out_new, rows_out)
+
+    energies = factors[0, 2]
+    for peer in range(1, 16):
+        energies = energies + factors[peer, 2]
 
     def limit(row):
-        parts = factors[0, row : row + 1, :]
-        for peer in range(1, 16):
-            parts = parts + factors[peer, row : row + 1, :]
-        energy = jnp.sum(parts, axis=1, keepdims=True)
+        energy = jnp.sum(energies[row : row + 1, :], axis=1, keepdims=True)
         return 1.0 / jnp.maximum(1.0, jnp.sqrt(energy * (1.0 / (D * FF))))
 
-    limit_in, limit_out = limit(10), limit(11)
+    limit_in, limit_out = limit(2), limit(3)
 
     def factor_in(half, tile):
-        return factors[(half * 2 + tile // 8) * 4 + my_x, pl.ds(tile % 8, 1), :]
+        return factors[(half * 2 + tile // 8) * 4 + my_x, tile // 4 % 2, pl.ds(tile % 4, 1), :]
 
     def factor_out(half, tile):
-        return factors[(half * 2 + tile // 2) * 4 + my_x, pl.ds(8 + tile % 2, 1), :]
+        return factors[(half * 2 + tile // 2) * 4 + my_x, 2, pl.ds(tile % 2, 1), :]
 
     def block(buffer, target, offset, width, start):
         write(
@@ -346,8 +315,8 @@
             factor = factor_in(half, tile)
             buf_cols[pl.ds(half * TILES_IN + tile, 1), :] = factor
             buf_in[which, :, lanes(tile)] = value(0, 0, tile) * (lax.rsqrt(factor) * limit_in)
-            if tile % 4 == 3:
-                block(buf_in.at[which], update_in, half * HALF_IN, 512, (tile - 3) * 128)
+            if tile % 8 == 7:
+                block(buf_in.at[which], update_in, half * HALF_IN, 1024, (tile - 7) * 128)
         for tile in range(TILES_OUT):
             factor = factor_out(half, tile)
             buf_cols[pl.ds(32 + half * TILES_OUT + tile, 1), :] = factor
@@ -358,6 +327,8 @@
                 )
             if tile % 2 == 1:
                 block(buf_out.at[which], update_out, half * HALF_OUT, 256, (tile - 1) * 128)
+    write(rows_in_new, rows_in)
+    write(rows_out_new, rows_out)
     write(buf_cols.at[0:32, :], cols_in)
     write(buf_cols.at[32:40, :], cols_out)
     for copy in copies:
@@ -381,7 +352,7 @@
             pltpu.VMEM((2, ROWS_IN, HALF_IN), F32),
             pltpu.VMEM((2, ROWS_OUT, HALF_OUT), F32),
             pltpu.VMEM((40, 128), F32),
-            pltpu.SemaphoreType.DMA((16,)),
+            pltpu.SemaphoreType.DMA((12,)),
         ],
         compiler_params=PARAMS,
         name="update",
@@ -394,22 +365,23 @@
 
 def per_device(grad_in, grad_out, rows_in, cols_in, rows_out, cols_out):
     swap = [(0, 1), (1, 0)]
-    grad_in, grad_out = keep_in_hbm(grad_in[0]), keep_in_hbm(grad_out[0])
-    first, own_in, own_out, rows_in, rows_out, cols_in, cols_out = fetch(
-        grad_in,
-        grad_out,
+    grad_in, grad_out = grad_in[0], grad_out[0]
+    grad_in_far, grad_out_far = keep_in_hbm(grad_in), keep_in_hbm(grad_out)
+    arrived_own = lax.ppermute(fetch(grad_in_far, grad_out_far), "dp", swap)
+    own = widen_own(grad_in, grad_out)
+    arrived_other = lax.ppermute(own, "dp", swap)
+
+    summed, row_sums = row_sums_of(own, arrived_own)
+    row_sums = lax.all_to_all(row_sums, ("dp", "x"), 0, 0)
+    other, rows_in, rows_out, cols_in, cols_out = add_other(
+        grad_in_far,
+        grad_out_far,
+        arrived_other,
         keep_in_hbm(rows_in.reshape(1, ROWS_IN)),
         keep_in_hbm(rows_out.reshape(1, ROWS_OUT)),
-        keep_in_hbm(cols_in.reshape(4, 8, 128)),
+        keep_in_hbm(cols_in.reshape(8, 4, 128)),
         keep_in_hbm(cols_out.reshape(4, 2, 128)),
     )
-    arrived_own = lax.ppermute(first, "dp", swap)
-    own = widen_own(own_in, own_out)
-    arrived_other = lax.ppermute(own, "dp", swap)
-
-    summed, row_sums = row_sums_of(own, arrived_own)
-    row_sums = lax.all_to_all(row_sums, ("dp", "x"), 0, 0)
-    other = add_other(grad_in, grad_out, arrived_other)
     scaled, row_scale, new_rows_in, new_rows_out, sums, other = column_sums_of(
         row_sums, rows_in, rows_out, summed, other
     )

time: 64 us -> 63.1 us (0.986)
  blocking collectives: 39.4 us -> 38.6 us
where the time goes in v4:
time: 63.1 us; the launch traced here: 62.8 us
  blocking collectives  38.6 us (61%)
  starting transfers between devices  14.3 us (23%)
  Pallas kernels  5.15 us (8%)
  waiting for transfers between devices  3.9 us (6%)
  between operations  0.72 us (1%)
    all_to_all x1, blocking collectives, per_device(): sums = lax.all_to_all(total_of(sums), 'z', 0, 0)  17.1 us
    all_to_all x1, blocking collectives, per_device(): lax.all_to_all(factors_of(sums, cols_in, cols_out), ('dp', 'pair', 'x'),...  11.8 us
    all_to_all x1, blocking collectives, per_device(): sums = lax.all_to_all(sums, ('y', 'pair'), 0, 0)  9.75 us
    ppermute x1, starting transfers between devices, per_device(): arrived_own = lax.ppermute(fetch(grad_in_far, grad_out_far), 'dp', swap)  8.79 us
    all_to_all x1, waiting for transfers between devices, per_device(): row_sums = lax.all_to_all(row_sums, ('dp', 'x'), 0, 0)  3.67 us
    all_to_all x1, starting transfers between devices, per_device(): row_sums = lax.all_to_all(row_sums, ('dp', 'x'), 0, 0)  3.63 us
    ppermute x1, starting transfers between devices, per_device(): arrived_other = lax.ppermute(own, 'dp', swap)  1.92 us
    pallas_call x1, Pallas kernels, update_of(): pl.pallas_call(update_kernel, out_shape=(jax.ShapeDtypeStruct((ROWS_IN, C...  1.55 us
  transfers between devices with their start and end apart: 3, of which 2 were waited for; matrix products, arithmetic and copies ran while one was open for 0% of the time, Pallas kernels for 3%

profile of v4, /device:TPU:1, one launch (start us, length us, event | category | flops | bytes accessed | tf_op | source)
XLA Modules:
  0.0 62.8 jit_solution(8139852007126311265)
XLA Ops:
  0.6 0.0 copy-start
  0.6 0.0 copy-start.1
  0.7 1.2 %fetch.1 = f32[128,2048]{1,0:T(8,128)S(1)} custom-call(bf16[64,4096]{1,0:T(8,128)(2,1)} %bitcast.10, bf16[256,1024]{1,0:T(8,128)(2,1)} %bitcast.13), custom_call_target="tpu_custom_call" | custom-call | tf_op jit(solution)/shard_map/fetch/pallas_call | solution.py:60
  1.8 8.8 %collective-permute-start = (f32[128,2048]{1,0:T(8,128)S(1)}, f32[128,2048]{1,0:T(8,128)S(1)}, u32[]{:S(2)}, u32[]{:S(2)}) collective-permute-start(f32[128,2048]{1,0:T(8,128)S(1)} %fetch.1), channel_id=1, source_target_pairs={{0,256},{256,0},{1,257},{257,1},{2,258},{258,2},{3,259},{259,3},{4... | collective-permute-start | bytes 3145736 | tf_op jit(solution)/shard_map/ppermute | solution.py:370
  10.6 0.0 copy-done
  10.6 0.0 copy-done.1
  10.7 0.1 widen_own.1.own
  10.7 1.9 %collective-permute-start.1 = (f32[128,2048]{1,0:T(8,128)S(1)}, f32[128,2048]{1,0:T(8,128)S(1)}, u32[]{:S(2)}, u32[]{:S(2)}) collective-permute-start(f32[128,2048]{1,0:T(8,128)S(1)} %widen_own.1.own), channel_id=1, source_target_pairs={{0,256},{256,0},{1,257},{257,1},{2,258},{258,2},{3,259},{259,3},{4... | collective-permute-start | bytes 3145736 | tf_op jit(solution)/shard_map/ppermute | solution.py:372
  12.7 0.2 collective-permute-done.received
  12.9 0.8 %row_sums.1 = (f32[128,2048]{1,0:T(8,128)S(1)}, f32[8,1,384]{2,1,0:T(1,128)}) custom-call(f32[128,2048]{1,0:T(8,128)S(1)} %widen_own.1.own, f32[128,2048]{1,0:T(8,128)S(1)} %collective-permute-done.received), custom_call_target="tpu_custom_call" | custom-call | tf_op jit(solution)/shard_map/row_sums/pallas_call | solution.py:146
  13.7 3.6 %all-to-all-start = ((f32[8,1,384]{2,1,0:T(1,128)}), f32[8,1,384]{2,1,0:T(1,128)S(1)}, u32[]{:S(2)}, u32[]{:S(2)}) async-start(f32[8,1,384]{2,1,0:T(1,128)} %get-tuple-element.25), calls=%async_computation | async-start | bytes 24576 | tf_op jit(solution)/shard_map/all_to_all | solution.py:375
  17.3 0.0 collective-permute-done.1.received
  17.3 1.2 %add_other.1 = (f32[128,2048]{1,0:T(8,128)S(1)}, f32[1,64]{1,0:T(1,128)S(1)}, f32[1,256]{1,0:T(1,128)S(1)}, f32[8,4,128]{2,1,0:T(4,128)S(1)}, f32[4,2,128]{2,1,0:T(2,128)S(1)}) custom-call(bf16[64,4096]{1,0:T(8,128)(2,1)} %bitcast.11, bf16[256,1024]{1,0:T(8,128)(2,1)} %bitcast.14, ...), custom_call_target="tpu_custom_call", output_to_operand_aliasing={{0}: (2, {})} | custom-call | flops 262144 | bytes 3145728 | tf_op jit(solution)/shard_map/add_other/pallas_call | solution.py:107
  18.5 3.7 %all-to-all-done.row_sums = f32[8,1,384]{2,1,0:T(1,128)S(1)} async-done(((f32[8,1,384]{2,1,0:T(1,128)}), f32[8,1,384]{2,1,0:T(1,128)S(1)}, u32[]{:S(2)}, u32[]{:S(2)}) %all-to-all-start) | async-done | bytes 12320 | tf_op jit(solution)/shard_map/all_to_all | solution.py:375
  22.2 0.3 column_sums.1
  22.5 9.7 %all_to_all.20.sums = f32[8,5,4,128]{3,2,1,0:T(4,128)S(1)} all-to-all(f32[8,5,4,128]{3,2,1,0:T(4,128)S(1)} %get-tuple-element.30), channel_id=1, replica_groups=mesh['dp'=2,'z'=8,'y'=4,'pair'=2,'x'=4] {'y','pair'}, dimensions={0} | all-to-all | bytes 163840 | tf_op jit(solution)/shard_map/all_to_all | solution.py:388
  32.3 17.1 %all_to_all.21.sums = f32[8,5,4,128]{3,2,1,0:T(4,128)S(1)} all-to-all(f32[8,5,4,128]{3,2,1,0:T(4,128)S(1)} %total.1), channel_id=1, replica_groups=mesh['dp'=2,'z'=8,'y'=4,'pair'=2,'x'=4] {'z'}, dimensions={0} | all-to-all | bytes 163840 | tf_op jit(solution)/shard_map/all_to_all | solution.py:389
  49.4 11.8 %all_to_all.22.factors = f32[16,3,4,128]{3,2,1,0:T(4,128)S(1)} all-to-all(f32[16,3,4,128]{3,2,1,0:T(4,128)S(1)} %column_factors.1), channel_id=1, replica_groups=mesh['dp'=2,'z'=8,'y'=4,'pair'=2,'x'=4] {'dp','pair','x'}, dimensions={0} | all-to-all | bytes 196608 | tf_op jit(solution)/shard_map/all_to_all | solution.py:390
  61.2 1.6 %update.1 = (f32[64,4096]{1,0:T(8,128)}, f32[256,1024]{1,0:T(8,128)}, f32[1,64]{1,0:T(1,128)}, f32[1,256]{1,0:T(1,128)}, f32[32,128]{1,0:T(8,128)}, /*index=5*/f32[8,128]{1,0:T(8,128)}) custom-call(f32[16,3,4,128]{3,2,1,0:T(4,128)S(1)} %all_to_all.22.factors, f32[128,2048]{1,0:T(8,128)S(1)} %get-tuple-element.33.scaled, ...), custom_call_target="tpu_custom_call" | custom-call | tf_op jit(solution)/shard_map/update/pallas_call | solution.py:339
  (2 shorter events, 0.1 us)
Async XLA Ops:
  0.6 10.0 %copy-start = (bf16[1,64,4096]{2,1,0:T(8,128)(2,1)S(1)}, bf16[1,64,4096]{2,1,0:T(8,128)(2,1)}, u32[]{:S(2)}) copy-start(bf16[1,64,4096]{2,1,0:T(8,128)(2,1)} %param.6) | copy-start | bytes 1572868
  0.6 10.0 %copy-start.1 = (bf16[1,256,1024]{2,1,0:T(8,128)(2,1)S(1)}, bf16[1,256,1024]{2,1,0:T(8,128)(2,1)}, u32[]{:S(2)}) copy-start(bf16[1,256,1024]{2,1,0:T(8,128)(2,1)} %param.7) | copy-start | bytes 1572868
  1.8 11.1 %collective-permute-start = (f32[128,2048]{1,0:T(8,128)S(1)}, f32[128,2048]{1,0:T(8,128)S(1)}, u32[]{:S(2)}, u32[]{:S(2)}) collective-permute-start(f32[128,2048]{1,0:T(8,128)S(1)} %fetch.1), channel_id=1, source_target_pairs={{0,256},{256,0},{1,257},{257,1},{2,258},{258,2},{3,259},{259,3},{4... | collective-permute-start | bytes 3145736 | tf_op jit(solution)/shard_map/ppermute | solution.py:370
  10.7 6.6 %collective-permute-start.1 = (f32[128,2048]{1,0:T(8,128)S(1)}, f32[128,2048]{1,0:T(8,128)S(1)}, u32[]{:S(2)}, u32[]{:S(2)}) collective-permute-start(f32[128,2048]{1,0:T(8,128)S(1)} %widen_own.1.own), channel_id=1, source_target_pairs={{0,256},{256,0},{1,257},{257,1},{2,258},{258,2},{3,259},{259,3},{4... | collective-permute-start | bytes 3145736 | tf_op jit(solution)/shard_map/ppermute | solution.py:372
  13.7 8.5 %all-to-all-start = ((f32[8,1,384]{2,1,0:T(1,128)}), f32[8,1,384]{2,1,0:T(1,128)S(1)}, u32[]{:S(2)}, u32[]{:S(2)}) async-start(f32[8,1,384]{2,1,0:T(1,128)} %get-tuple-element.25), calls=%async_computation | async-start | bytes 24576 | tf_op jit(solution)/shard_map/all_to_all | solution.py:375

commit v5 on v4

--- a/solution.py
+++ b/solution.py
@@ -22,7 +22,6 @@
 F32 = jnp.float32
 VMEM = pl.BlockSpec(memory_space=pltpu.VMEM)
 HBM = pl.BlockSpec(memory_space=pltpu.HBM)
-ANY = pl.BlockSpec(memory_space=pl.ANY)
 PARAMS = pltpu.CompilerParams(vmem_limit_bytes=16 * 1024 * 1024)
 
 
@@ -45,27 +44,31 @@
 ]
 
 
-def fetch_kernel(grad_in, grad_out, other, other_in, other_out, sems):
+def fetch_kernel(grad_in, grad_out, *refs):
+    first, other_in, other_out, sems = refs[4], refs[9], refs[10], refs[11]
     copies = half_copies(grad_in, grad_out, 1 - lax.axis_index("dp"), other_in, other_out, sems)
-    for copy in copies:
+    small = [pltpu.make_async_copy(refs[at], refs[5 + at], sems.at[2 + at]) for at in range(4)]
+    for copy in (*copies, *small):
         copy.start()
     copies[0].wait()
-    other[0:64, :] = other_in[...].astype(F32)
+    first[0:64, :] = other_in[...].astype(F32)
     copies[1].wait()
     for k in range(BLOCKS):
-        other[64:128, pl.ds(k * HALF_OUT, HALF_OUT)] = other_out[pl.ds(64 * k, 64), :].astype(F32)
-
-
-def fetch(grad_in, grad_out):
+        first[64:128, pl.ds(k * HALF_OUT, HALF_OUT)] = other_out[pl.ds(64 * k, 64), :].astype(F32)
+    for copy in small:
+        copy.wait()
+
+
+def fetch(grad_in, grad_out, *factors):
     return pl.pallas_call(
         fetch_kernel,
-        out_shape=jax.ShapeDtypeStruct(PACK, F32),
-        in_specs=[HBM, HBM],
-        out_specs=VMEM,
-        scratch_shapes=HALF_SCRATCH + [pltpu.SemaphoreType.DMA((2,))],
+        out_shape=tuple(jax.ShapeDtypeStruct(shape, F32) for shape in (PACK, *(x.shape for x in factors))),
+        in_specs=[HBM] * 6,
+        out_specs=(VMEM,) * 5,
+        scratch_shapes=HALF_SCRATCH + [pltpu.SemaphoreType.DMA((6,))],
         compiler_params=PARAMS,
         name="fetch",
-    )(grad_in, grad_out)
+    )(grad_in, grad_out, *factors)
 
 
 def widen_kernel(grad_in, grad_out, packed):
@@ -80,41 +83,11 @@
     return pl.pallas_call(
         widen_kernel,
         out_shape=jax.ShapeDtypeStruct(PACK, F32),
-        in_specs=[VMEM, VMEM],
+        in_specs=[VMEM] * 2,
         out_specs=VMEM,
         compiler_params=PARAMS,
         name="widen_own",
     )(grad_in, grad_out)
-
-
-def add_kernel(grad_in, grad_out, received, *refs):
-    total, other_in, other_out, sems = refs[4], refs[9], refs[10], refs[11]
-    copies = half_copies(grad_in, grad_out, 1 - lax.axis_index("dp"), other_in, other_out, sems)
-    small = [pltpu.make_async_copy(refs[at], refs[5 + at], sems.at[2 + at]) for at in range(4)]
-    for copy in (*copies, *small):
-        copy.start()
-    copies[0].wait()
-    total[0:64, :] = received[0:64, :] + other_in[...].astype(F32)
-    copies[1].wait()
-    for k in range(BLOCKS):
-        block = pl.ds(k * HALF_OUT, HALF_OUT)
-        total[64:128, block] = received[64:128, block] + other_out[pl.ds(64 * k, 64), :].astype(F32)
-    for copy in small:
-        copy.wait()
-
-
-def add_other(grad_in, grad_out, received, *factors):
-    return pl.pallas_call(
-        add_kernel,
-        out_shape=tuple(jax.ShapeDtypeStruct(x.shape, F32) for x in (received, *factors)),
-        in_specs=[HBM, HBM, VMEM] + [HBM] * 4,
-        out_specs=(VMEM,) * 5,
-        scratch_shapes=HALF_SCRATCH + [pltpu.SemaphoreType.DMA((6,))],
-        input_output_aliases={2: 0},
-        cost_estimate=pl.CostEstimate(flops=262144, bytes_accessed=3 * 1024 * 1024, transcendentals=0),
-        compiler_params=pltpu.CompilerParams(vmem_limit_bytes=4 * 1024 * 1024),
-        name="add_other",
-    )(grad_in, grad_out, received, *factors)
 
 
 def rows_kernel(own, received, summed, row_sums):
@@ -153,10 +126,7 @@
     )(own, received)
 
 
-def columns_kernel(
-    row_sums, rows_in, rows_out, summed, other, scaled, row_scale, new_in, new_out, sends, other_on
-):
-    del other, other_on
+def columns_kernel(row_sums, rows_in, rows_out, summed, scaled, row_scale, new_in, new_out, sends):
     total = jnp.sum(row_sums[...], axis=0)
     fresh_in = DECAY * rows_in[...] + (1.0 - DECAY) * (total[:, 0:64] * (1.0 / FF) + EPSILON)
     fresh_out = DECAY * rows_out[...] + (1.0 - DECAY) * (total[:, 128:384] * (1.0 / D) + EPSILON)
@@ -201,7 +171,7 @@
         send(tile // 2, 18 + tile % 2, fold(weighted))
 
 
-def column_sums_of(row_sums, rows_in, rows_out, summed, other):
+def column_sums_of(row_sums, rows_in, rows_out, summed):
     return pl.pallas_call(
         columns_kernel,
         out_shape=(
@@ -210,14 +180,12 @@
             jax.ShapeDtypeStruct((1, ROWS_IN), F32),
             jax.ShapeDtypeStruct((1, ROWS_OUT), F32),
             jax.ShapeDtypeStruct((8, 5, 4, 128), F32),
-            jax.ShapeDtypeStruct(PACK, F32),
         ),
-        in_specs=[VMEM] * 4 + [ANY],
-        out_specs=(VMEM,) * 5 + (ANY,),
-        input_output_aliases={4: 5},
+        in_specs=[VMEM] * 4,
+        out_specs=(VMEM,) * 5,
         compiler_params=PARAMS,
         name="column_sums",
-    )(row_sums, rows_in, rows_out, summed, other)
+    )(row_sums, rows_in, rows_out, summed)
 
 
 def total_kernel(sums, sends):
@@ -268,36 +236,51 @@
     )(sums, cols_in, cols_out)
 
 
+def scales_kernel(factors, cols, scales):
+    my_x = lax.axis_index("x")
+    energies = factors[0, 2]
+    for peer in range(1, 16):
+        energies = energies + factors[peer, 2]
+
+    def limit(row):
+        energy = jnp.sum(energies[row : row + 1, :], axis=1, keepdims=True)
+        return 1.0 / jnp.maximum(1.0, jnp.sqrt(energy * (1.0 / (D * FF))))
+
+    limit_in, limit_out = limit(2), limit(3)
+    for chunk in range(4):
+        owner = chunk * 4 + my_x
+        for part in range(2):
+            here = factors[owner, part]
+            cols[pl.ds(chunk * 8 + part * 4, 4), :] = here
+            scales[pl.ds(chunk * 8 + part * 4, 4), :] = lax.rsqrt(here) * limit_in
+        here = factors[owner, 2, 0:2, :]
+        cols[pl.ds(32 + chunk * 2, 2), :] = here
+        scales[pl.ds(32 + chunk * 2, 2), :] = lax.rsqrt(here) * limit_out
+
+
+def scales_of(factors):
+    return pl.pallas_call(
+        scales_kernel,
+        out_shape=(jax.ShapeDtypeStruct((40, 128), F32), jax.ShapeDtypeStruct((40, 128), F32)),
+        in_specs=[VMEM],
+        out_specs=(VMEM, VMEM),
+        compiler_params=PARAMS,
+        name="scales",
+    )(factors)
+
+
 def update_kernel(
-    factors, scaled, row_scale, other, rows_in_new, rows_out_new,
+    cols, scales, scaled, row_scale, first, received, rows_in_new, rows_out_new,
     update_in, update_out, rows_in, rows_out, cols_in, cols_out,
-    buf_in, buf_out, buf_cols, sems,
+    buf_in, buf_out, sems,
 ):
     own_half = lax.axis_index("dp")
-    my_x = lax.axis_index("x")
     copies = []
 
     def write(source, target):
         copy = pltpu.make_async_copy(source, target, sems.at[len(copies)])
         copy.start()
         copies.append(copy)
-
-
-    energies = factors[0, 2]
-    for peer in range(1, 16):
-        energies = energies + factors[peer, 2]
-
-    def limit(row):
-        energy = jnp.sum(energies[row : row + 1, :], axis=1, keepdims=True)
-        return 1.0 / jnp.maximum(1.0, jnp.sqrt(energy * (1.0 / (D * FF))))
-
-    limit_in, limit_out = limit(2), limit(3)
-
-    def factor_in(half, tile):
-        return factors[(half * 2 + tile // 8) * 4 + my_x, tile // 4 % 2, pl.ds(tile % 4, 1), :]
-
-    def factor_out(half, tile):
-        return factors[(half * 2 + tile // 2) * 4 + my_x, 2, pl.ds(tile % 2, 1), :]
 
     def block(buffer, target, offset, width, start):
         write(
@@ -305,37 +288,35 @@
             target.at[:, pl.ds(pl.multiple_of(offset + start, 128), width)],
         )
 
-    for which, half, source in ((0, own_half, scaled), (1, 1 - own_half, other)):
+    write(cols.at[0:32, :], cols_in)
+    write(cols.at[32:40, :], cols_out)
+    write(rows_in_new, rows_in)
+    write(rows_out_new, rows_out)
+    for which, half in ((0, own_half), (1, 1 - own_half)):
 
         def value(row, scale_row, tile):
-            rows = source[pl.ds(row, 64), lanes(tile)]
-            return rows if which == 0 else rows * row_scale[pl.ds(scale_row, 64), :]
+            if which == 0:
+                return scaled[pl.ds(row, 64), lanes(tile)]
+            both = first[pl.ds(row, 64), lanes(tile)] + received[pl.ds(row, 64), lanes(tile)]
+            return both * row_scale[pl.ds(scale_row, 64), :]
 
         for tile in range(TILES_IN):
-            factor = factor_in(half, tile)
-            buf_cols[pl.ds(half * TILES_IN + tile, 1), :] = factor
-            buf_in[which, :, lanes(tile)] = value(0, 0, tile) * (lax.rsqrt(factor) * limit_in)
+            buf_in[which, :, lanes(tile)] = value(0, 0, tile) * scales[pl.ds(half * TILES_IN + tile, 1), :]
             if tile % 8 == 7:
                 block(buf_in.at[which], update_in, half * HALF_IN, 1024, (tile - 7) * 128)
         for tile in range(TILES_OUT):
-            factor = factor_out(half, tile)
-            buf_cols[pl.ds(32 + half * TILES_OUT + tile, 1), :] = factor
-            scale = lax.rsqrt(factor) * limit_out
+            scale = scales[pl.ds(32 + half * TILES_OUT + tile, 1), :]
             for k in range(BLOCKS):
                 buf_out[which, pl.ds(64 * k, 64), lanes(tile)] = (
                     value(64, 64 + 64 * k, k * TILES_OUT + tile) * scale
                 )
             if tile % 2 == 1:
                 block(buf_out.at[which], update_out, half * HALF_OUT, 256, (tile - 1) * 128)
-    write(rows_in_new, rows_in)
-    write(rows_out_new, rows_out)
-    write(buf_cols.at[0:32, :], cols_in)
-    write(buf_cols.at[32:40, :], cols_out)
     for copy in copies:
         copy.wait()
 
 
-def update_of(factors, scaled, row_scale, other, rows_in_new, rows_out_new):
+def update_of(*operands):
     return pl.pallas_call(
         update_kernel,
         out_shape=(
@@ -346,17 +327,16 @@
             jax.ShapeDtypeStruct((COLS_IN // 128, 128), F32),
             jax.ShapeDtypeStruct((COLS_OUT // 128, 128), F32),
         ),
-        in_specs=[VMEM] * 6,
+        in_specs=[VMEM] * 8,
         out_specs=(HBM,) * 6,
         scratch_shapes=[
             pltpu.VMEM((2, ROWS_IN, HALF_IN), F32),
             pltpu.VMEM((2, ROWS_OUT, HALF_OUT), F32),
-            pltpu.VMEM((40, 128), F32),
             pltpu.SemaphoreType.DMA((12,)),
         ],
         compiler_params=PARAMS,
         name="update",
-    )(factors, scaled, row_scale, other, rows_in_new, rows_out_new)
+    )(*operands)
 
 
 def keep_in_hbm(x):
@@ -366,30 +346,32 @@
 def per_device(grad_in, grad_out, rows_in, cols_in, rows_out, cols_out):
     swap = [(0, 1), (1, 0)]
     grad_in, grad_out = grad_in[0], grad_out[0]
-    grad_in_far, grad_out_far = keep_in_hbm(grad_in), keep_in_hbm(grad_out)
-    arrived_own = lax.ppermute(fetch(grad_in_far, grad_out_far), "dp", swap)
+    first, rows_in, rows_out, cols_in, cols_out = fetch(
+        *map(
+            keep_in_hbm,
+            (
+                grad_in,
+                grad_out,
+                rows_in.reshape(1, ROWS_IN),
+                rows_out.reshape(1, ROWS_OUT),
+                cols_in.reshape(8, 4, 128),
+                cols_out.reshape(4, 2, 128),
+            ),
+        )
+    )
+    arrived_own = lax.ppermute(first, "dp", swap)
     own = widen_own(grad_in, grad_out)
     arrived_other = lax.ppermute(own, "dp", swap)
 
     summed, row_sums = row_sums_of(own, arrived_own)
     row_sums = lax.all_to_all(row_sums, ("dp", "x"), 0, 0)
-    other, rows_in, rows_out, cols_in, cols_out = add_other(
-        grad_in_far,
-        grad_out_far,
-        arrived_other,
-        keep_in_hbm(rows_in.reshape(1, ROWS_IN)),
-        keep_in_hbm(rows_out.reshape(1, ROWS_OUT)),
-        keep_in_hbm(cols_in.reshape(8, 4, 128)),
-        keep_in_hbm(cols_out.reshape(4, 2, 128)),
-    )
-    scaled, row_scale, new_rows_in, new_rows_out, sums, other = column_sums_of(
-        row_sums, rows_in, rows_out, summed, other
-    )
+    scaled, row_scale, new_rows_in, new_rows_out, sums = column_sums_of(row_sums, rows_in, rows_out, summed)
     sums = lax.all_to_all(sums, ("y", "pair"), 0, 0)
     sums = lax.all_to_all(total_of(sums), "z", 0, 0)
     factors = lax.all_to_all(factors_of(sums, cols_in, cols_out), ("dp", "pair", "x"), 0, 0)
+    cols, scales = scales_of(factors)
     update_in, update_out, new_rows_in, new_rows_out, new_cols_in, new_cols_out = update_of(
-        factors, scaled, row_scale, other, new_rows_in, new_rows_out
+        cols, scales, scaled, row_scale, first, arrived_other, new_rows_in, new_rows_out
     )
     return (
         update_in,

time: 63.1 us -> 62.4 us (0.989)
  blocking collectives: 38.6 us -> 46.9 us
  waiting for transfers between devices: 3.9 us -> 0.23 us
  starting transfers between devices: 14.3 us -> 10.7 us
  Pallas kernels: 5.15 us -> 3.44 us
    all_to_all x0 -> x1, blocking collectives: none -> 7.62 us  [per_device(): row_sums = lax.all_to_all(row_sums, ('dp', 'x'), 0, 0)]
    all_to_all x1 -> x0, waiting for transfers between devices: 3.67 us -> none  [per_device(): row_sums = lax.all_to_all(row_sums, ('dp', 'x'), 0, 0)]
    all_to_all x1 -> x0, starting transfers between devices: 3.63 us -> none  [per_device(): row_sums = lax.all_to_all(row_sums, ('dp', 'x'), 0, 0)]
    pallas_call x2, Pallas kernels: 2.38 us -> 1.33 us  [the longest x1 1.22 us: fetch(): pl.pallas_call(fetch_kernel, out_shape=tuple((jax.ShapeDtypeStruct(shape,...]
  transfers between devices with their start and end apart: 3 -> 2, of which waited for: 2 -> 1; matrix products, arithmetic and copies ran while one was open for 0% -> 0% of each run, Pallas kernels for 3% -> 1%
where the time goes in v5:
time: 62.4 us; the launch traced here: 62.1 us
  blocking collectives  46.9 us (75%)
  starting transfers between devices  10.7 us (17%)
  Pallas kernels  3.44 us (6%)
  between operations  0.73 us (1%)
    all_to_all x1, blocking collectives, per_device(): sums = lax.all_to_all(total_of(sums), 'z', 0, 0)  17.2 us
    all_to_all x1, blocking collectives, per_device(): lax.all_to_all(factors_of(sums, cols_in, cols_out), ('dp', 'pair', 'x'),...  11.8 us
    all_to_all x1, blocking collectives, per_device(): sums = lax.all_to_all(sums, ('y', 'pair'), 0, 0)  10.3 us
    ppermute x1, starting transfers between devices, per_device(): arrived_own = lax.ppermute(first, 'dp', swap)  8.79 us
    all_to_all x1, blocking collectives, per_device(): row_sums = lax.all_to_all(row_sums, ('dp', 'x'), 0, 0)  7.62 us
    ppermute x1, starting transfers between devices, per_device(): arrived_other = lax.ppermute(own, 'dp', swap)  1.92 us
    pallas_call x1, Pallas kernels, update_of(): pl.pallas_call(update_kernel, out_shape=(jax.ShapeDtypeStruct((ROWS_IN, C...  1.45 us
  transfers between devices with their start and end apart: 2, of which 1 were waited for; matrix products, arithmetic and copies ran while one was open for 0% of the time, Pallas kernels for 1%

profile of v5, /device:TPU:1, one launch (start us, length us, event | category | flops | bytes accessed | tf_op | source)
XLA Modules:
  0.0 62.1 jit_solution(16854155432264430374)
XLA Ops:
  0.6 0.0 copy-start
  0.6 0.0 copy-start.1
  0.7 1.2 %fetch.1 = (f32[128,2048]{1,0:T(8,128)S(1)}, f32[1,64]{1,0:T(1,128)S(1)}, f32[1,256]{1,0:T(1,128)S(1)}, f32[8,4,128]{2,1,0:T(4,128)S(1)}, f32[4,2,128]{2,1,0:T(2,128)S(1)}) custom-call(bf16[64,4096]{1,0:T(8,128)(2,1)} %bitcast.10, bf16[256,1024]{1,0:T(8,128)(2,1)} %bitcast.12, f32[1,64]{1,0:T(1,128)} %bitcast.17, f32[1,256]{1,0:T(1,128)} %bitcast.16, ...), custom_call_target="tpu_custom_call" | custom-call | tf_op jit(solution)/shard_map/fetch/pallas_call | solution.py:63
  1.9 8.8 %collective-permute-start = (f32[128,2048]{1,0:T(8,128)S(1)}, f32[128,2048]{1,0:T(8,128)S(1)}, u32[]{:S(2)}, u32[]{:S(2)}) collective-permute-start(f32[128,2048]{1,0:T(8,128)S(1)} %get-tuple-element.26.first), channel_id=1, source_target_pairs={{0,256},{256,0},{1,257},{257,1},{2,258},{258,2},{3,259},{259,3},{4... | collective-permute-start | bytes 3145736 | tf_op jit(solution)/shard_map/ppermute | solution.py:362
  10.7 0.0 copy-done
  10.7 0.0 copy-done.1
  10.7 0.1 widen_own.1.own
  10.8 1.9 %collective-permute-start.1 = (f32[128,2048]{1,0:T(8,128)S(1)}, f32[128,2048]{1,0:T(8,128)S(1)}, u32[]{:S(2)}, u32[]{:S(2)}) collective-permute-start(f32[128,2048]{1,0:T(8,128)S(1)} %widen_own.1.own), channel_id=1, source_target_pairs={{0,256},{256,0},{1,257},{257,1},{2,258},{258,2},{3,259},{259,3},{4... | collective-permute-start | bytes 3145736 | tf_op jit(solution)/shard_map/ppermute | solution.py:364
  12.7 0.2 collective-permute-done.received
  12.9 0.2 row_sums.1
  13.2 7.6 %all_to_all.20.row_sums = f32[8,1,384]{2,1,0:T(1,128)S(1)} all-to-all(f32[8,1,384]{2,1,0:T(1,128)S(1)} %get-tuple-element.27), channel_id=1, replica_groups=mesh['dp'=2,'z'=8,'y'=4,'pair'=2,'x'=4] {'dp','x'}, dimensions={0} | all-to-all | bytes 24576 | tf_op jit(solution)/shard_map/all_to_all | solution.py:367
  20.8 0.3 column_sums.1
  21.1 10.3 %all_to_all.21.sums = f32[8,5,4,128]{3,2,1,0:T(4,128)S(1)} all-to-all(f32[8,5,4,128]{3,2,1,0:T(4,128)S(1)} %get-tuple-element.31), channel_id=1, replica_groups=mesh['dp'=2,'z'=8,'y'=4,'pair'=2,'x'=4] {'y','pair'}, dimensions={0} | all-to-all | bytes 163840 | tf_op jit(solution)/shard_map/all_to_all | solution.py:369
  31.4 17.2 %all_to_all.22.sums = f32[8,5,4,128]{3,2,1,0:T(4,128)S(1)} all-to-all(f32[8,5,4,128]{3,2,1,0:T(4,128)S(1)} %total.1), channel_id=1, replica_groups=mesh['dp'=2,'z'=8,'y'=4,'pair'=2,'x'=4] {'z'}, dimensions={0} | all-to-all | bytes 163840 | tf_op jit(solution)/shard_map/all_to_all | solution.py:370
  48.7 11.8 %all_to_all.23.factors = f32[16,3,4,128]{3,2,1,0:T(4,128)S(1)} all-to-all(f32[16,3,4,128]{3,2,1,0:T(4,128)S(1)} %column_factors.1), channel_id=1, replica_groups=mesh['dp'=2,'z'=8,'y'=4,'pair'=2,'x'=4] {'dp','pair','x'}, dimensions={0} | all-to-all | bytes 196608 | tf_op jit(solution)/shard_map/all_to_all | solution.py:371
  60.5 0.1 scales.1
  60.6 0.0 collective-permute-done.1.received
  60.6 1.4 %update.1 = (f32[64,4096]{1,0:T(8,128)}, f32[256,1024]{1,0:T(8,128)}, f32[1,64]{1,0:T(1,128)}, f32[1,256]{1,0:T(1,128)}, f32[32,128]{1,0:T(8,128)}, /*index=5*/f32[8,128]{1,0:T(8,128)}) custom-call(f32[40,128]{1,0:T(8,128)S(1)} %get-tuple-element.34.cols, f32[40,128]{1,0:T(8,128)S(1)} %get-tuple-element.35.scales, f32[128,2048]{1,0:T(8,128)S(1)} %get-tuple-element.36.scaled, ...), custom_call_target="tpu_custom_call" | custom-call | tf_op jit(solution)/shard_map/update/pallas_call | solution.py:320
  (2 shorter events, 0.1 us)
Async XLA Ops:
  0.6 10.0 %copy-start = (bf16[1,64,4096]{2,1,0:T(8,128)(2,1)S(1)}, bf16[1,64,4096]{2,1,0:T(8,128)(2,1)}, u32[]{:S(2)}) copy-start(bf16[1,64,4096]{2,1,0:T(8,128)(2,1)} %param.6) | copy-start | bytes 1572868
  0.6 10.0 %copy-start.1 = (bf16[1,256,1024]{2,1,0:T(8,128)(2,1)S(1)}, bf16[1,256,1024]{2,1,0:T(8,128)(2,1)}, u32[]{:S(2)}) copy-start(bf16[1,256,1024]{2,1,0:T(8,128)(2,1)} %param.7) | copy-start | bytes 1572868
  1.9 11.1 %collective-permute-start = (f32[128,2048]{1,0:T(8,128)S(1)}, f32[128,2048]{1,0:T(8,128)S(1)}, u32[]{:S(2)}, u32[]{:S(2)}) collective-permute-start(f32[128,2048]{1,0:T(8,128)S(1)} %get-tuple-element.26.first), channel_id=1, source_target_pairs={{0,256},{256,0},{1,257},{257,1},{2,258},{258,2},{3,259},{259,3},{4... | collective-permute-start | bytes 3145736 | tf_op jit(solution)/shard_map/ppermute | solution.py:362
  10.8 49.8 %collective-permute-start.1 = (f32[128,2048]{1,0:T(8,128)S(1)}, f32[128,2048]{1,0:T(8,128)S(1)}, u32[]{:S(2)}, u32[]{:S(2)}) collective-permute-start(f32[128,2048]{1,0:T(8,128)S(1)} %widen_own.1.own), channel_id=1, source_target_pairs={{0,256},{256,0},{1,257},{257,1},{2,258},{258,2},{3,259},{259,3},{4... | collective-permute-start | bytes 3145736 | tf_op jit(solution)/shard_map/ppermute | solution.py:364

commit v6 on v5

--- a/solution.py
+++ b/solution.py
@@ -155,7 +155,7 @@
         return jnp.sum(value, axis=0, keepdims=True)
 
     def send(chunk, row, vector):
-        for peer in range(chunk, 8, 2):
+        for peer in range(4 * chunk, 4 * chunk + 4):
             sends[peer, row // 4, row % 4 : row % 4 + 1, :] = vector
 
     for tile in range(TILES_IN):
@@ -248,7 +248,7 @@
 
     limit_in, limit_out = limit(2), limit(3)
     for chunk in range(4):
-        owner = chunk * 4 + my_x
+        owner = my_x * 4 + chunk % 2 * 2 + chunk // 2
         for part in range(2):
             here = factors[owner, part]
             cols[pl.ds(chunk * 8 + part * 4, 4), :] = here
@@ -364,11 +364,11 @@
     arrived_other = lax.ppermute(own, "dp", swap)
 
     summed, row_sums = row_sums_of(own, arrived_own)
-    row_sums = lax.all_to_all(row_sums, ("dp", "x"), 0, 0)
+    row_sums = lax.all_to_all(row_sums, ("x", "dp"), 0, 0)
     scaled, row_scale, new_rows_in, new_rows_out, sums = column_sums_of(row_sums, rows_in, rows_out, summed)
-    sums = lax.all_to_all(sums, ("y", "pair"), 0, 0)
+    sums = lax.all_to_all(sums, ("pair", "y"), 0, 0)
     sums = lax.all_to_all(total_of(sums), "z", 0, 0)
-    factors = lax.all_to_all(factors_of(sums, cols_in, cols_out), ("dp", "pair", "x"), 0, 0)
+    factors = lax.all_to_all(factors_of(sums, cols_in, cols_out), ("x", "pair", "dp"), 0, 0)
     cols, scales = scales_of(factors)
     update_in, update_out, new_rows_in, new_rows_out, new_cols_in, new_cols_out = update_of(
         cols, scales, scaled, row_scale, first, arrived_other, new_rows_in, new_rows_out

time: 62.4 us -> 62.1 us (level)
  no operation moved by 1% of the time
where the time goes in v6:
time: 62.1 us; the launch traced here: 61.8 us
  blocking collectives  46.6 us (75%)
  starting transfers between devices  10.7 us (17%)
  Pallas kernels  3.44 us (6%)
  between operations  0.73 us (1%)
    all_to_all x1, blocking collectives, per_device(): sums = lax.all_to_all(total_of(sums), 'z', 0, 0)  17.2 us
    all_to_all x1, blocking collectives, per_device(): lax.all_to_all(factors_of(sums, cols_in, cols_out), ('x', 'pair', 'dp'),...  12.2 us
    all_to_all x1, blocking collectives, per_device(): sums = lax.all_to_all(sums, ('pair', 'y'), 0, 0)  9.8 us
    ppermute x1, starting transfers between devices, per_device(): arrived_own = lax.ppermute(first, 'dp', swap)  8.79 us
    all_to_all x1, blocking collectives, per_device(): row_sums = lax.all_to_all(row_sums, ('x', 'dp'), 0, 0)  7.36 us
    ppermute x1, starting transfers between devices, per_device(): arrived_other = lax.ppermute(own, 'dp', swap)  1.92 us
    pallas_call x1, Pallas kernels, update_of(): pl.pallas_call(update_kernel, out_shape=(jax.ShapeDtypeStruct((ROWS_IN, C...  1.45 us
  transfers between devices with their start and end apart: 2, of which 1 were waited for; matrix products, arithmetic and copies ran while one was open for 0% of the time, Pallas kernels for 1%

profile of v6, /device:TPU:1, one launch (start us, length us, event | category | flops | bytes accessed | tf_op | source)
XLA Modules:
  0.0 61.8 jit_solution(17157182417087291374)
XLA Ops:
  0.6 0.0 copy-start
  0.6 0.0 copy-start.1
  0.7 1.2 %fetch.1 = (f32[128,2048]{1,0:T(8,128)S(1)}, f32[1,64]{1,0:T(1,128)S(1)}, f32[1,256]{1,0:T(1,128)S(1)}, f32[8,4,128]{2,1,0:T(4,128)S(1)}, f32[4,2,128]{2,1,0:T(2,128)S(1)}) custom-call(bf16[64,4096]{1,0:T(8,128)(2,1)} %bitcast.10, bf16[256,1024]{1,0:T(8,128)(2,1)} %bitcast.12, f32[1,64]{1,0:T(1,128)} %bitcast.17, f32[1,256]{1,0:T(1,128)} %bitcast.16, ...), custom_call_target="tpu_custom_call" | custom-call | tf_op jit(solution)/shard_map/fetch/pallas_call | solution.py:63
  1.9 8.8 %collective-permute-start = (f32[128,2048]{1,0:T(8,128)S(1)}, f32[128,2048]{1,0:T(8,128)S(1)}, u32[]{:S(2)}, u32[]{:S(2)}) collective-permute-start(f32[128,2048]{1,0:T(8,128)S(1)} %get-tuple-element.26.first), channel_id=1, source_target_pairs={{0,256},{256,0},{1,257},{257,1},{2,258},{258,2},{3,259},{259,3},{4... | collective-permute-start | bytes 3145736 | tf_op jit(solution)/shard_map/ppermute | solution.py:362
  10.7 0.0 copy-done
  10.7 0.0 copy-done.1
  10.7 0.1 widen_own.1.own
  10.8 1.9 %collective-permute-start.1 = (f32[128,2048]{1,0:T(8,128)S(1)}, f32[128,2048]{1,0:T(8,128)S(1)}, u32[]{:S(2)}, u32[]{:S(2)}) collective-permute-start(f32[128,2048]{1,0:T(8,128)S(1)} %widen_own.1.own), channel_id=1, source_target_pairs={{0,256},{256,0},{1,257},{257,1},{2,258},{258,2},{3,259},{259,3},{4... | collective-permute-start | bytes 3145736 | tf_op jit(solution)/shard_map/ppermute | solution.py:364
  12.7 0.2 collective-permute-done.received
  12.9 0.2 row_sums.1
  13.2 7.4 %all_to_all.20.row_sums = f32[8,1,384]{2,1,0:T(1,128)S(1)} all-to-all(f32[8,1,384]{2,1,0:T(1,128)S(1)} %get-tuple-element.27), channel_id=1, replica_groups=mesh['dp'=2,'z'=8,'y'=4,'pair'=2,'x'=4] {'x','dp'}, dimensions={0} | all-to-all | bytes 24576 | tf_op jit(solution)/shard_map/all_to_all | solution.py:367
  20.5 0.3 column_sums.1
  20.8 9.8 %all_to_all.21.sums = f32[8,5,4,128]{3,2,1,0:T(4,128)S(1)} all-to-all(f32[8,5,4,128]{3,2,1,0:T(4,128)S(1)} %get-tuple-element.31), channel_id=1, replica_groups=mesh['dp'=2,'z'=8,'y'=4,'pair'=2,'x'=4] {'pair','y'}, dimensions={0} | all-to-all | bytes 163840 | tf_op jit(solution)/shard_map/all_to_all | solution.py:369
  30.7 17.2 %all_to_all.22.sums = f32[8,5,4,128]{3,2,1,0:T(4,128)S(1)} all-to-all(f32[8,5,4,128]{3,2,1,0:T(4,128)S(1)} %total.1), channel_id=1, replica_groups=mesh['dp'=2,'z'=8,'y'=4,'pair'=2,'x'=4] {'z'}, dimensions={0} | all-to-all | bytes 163840 | tf_op jit(solution)/shard_map/all_to_all | solution.py:370
  47.9 12.2 %all_to_all.23.factors = f32[16,3,4,128]{3,2,1,0:T(4,128)S(1)} all-to-all(f32[16,3,4,128]{3,2,1,0:T(4,128)S(1)} %column_factors.1), channel_id=1, replica_groups=mesh['dp'=2,'z'=8,'y'=4,'pair'=2,'x'=4] {'x','pair','dp'}, dimensions={0} | all-to-all | bytes 196608 | tf_op jit(solution)/shard_map/all_to_all | solution.py:371
  60.2 0.1 scales.1
  60.3 0.0 collective-permute-done.1.received
  60.3 1.4 %update.1 = (f32[64,4096]{1,0:T(8,128)}, f32[256,1024]{1,0:T(8,128)}, f32[1,64]{1,0:T(1,128)}, f32[1,256]{1,0:T(1,128)}, f32[32,128]{1,0:T(8,128)}, /*index=5*/f32[8,128]{1,0:T(8,128)}) custom-call(f32[40,128]{1,0:T(8,128)S(1)} %get-tuple-element.34.cols, f32[40,128]{1,0:T(8,128)S(1)} %get-tuple-element.35.scales, f32[128,2048]{1,0:T(8,128)S(1)} %get-tuple-element.36.scaled, ...), custom_call_target="tpu_custom_call" | custom-call | tf_op jit(solution)/shard_map/update/pallas_call | solution.py:320
  (2 shorter events, 0.1 us)
Async XLA Ops:
  0.6 10.0 %copy-start = (bf16[1,64,4096]{2,1,0:T(8,128)(2,1)S(1)}, bf16[1,64,4096]{2,1,0:T(8,128)(2,1)}, u32[]{:S(2)}) copy-start(bf16[1,64,4096]{2,1,0:T(8,128)(2,1)} %param.6) | copy-start | bytes 1572868
  0.6 10.0 %copy-start.1 = (bf16[1,256,1024]{2,1,0:T(8,128)(2,1)S(1)}, bf16[1,256,1024]{2,1,0:T(8,128)(2,1)}, u32[]{:S(2)}) copy-start(bf16[1,256,1024]{2,1,0:T(8,128)(2,1)} %param.7) | copy-start | bytes 1572868
  1.9 11.1 %collective-permute-start = (f32[128,2048]{1,0:T(8,128)S(1)}, f32[128,2048]{1,0:T(8,128)S(1)}, u32[]{:S(2)}, u32[]{:S(2)}) collective-permute-start(f32[128,2048]{1,0:T(8,128)S(1)} %get-tuple-element.26.first), channel_id=1, source_target_pairs={{0,256},{256,0},{1,257},{257,1},{2,258},{258,2},{3,259},{259,3},{4... | collective-permute-start | bytes 3145736 | tf_op jit(solution)/shard_map/ppermute | solution.py:362
  10.8 49.5 %collective-permute-start.1 = (f32[128,2048]{1,0:T(8,128)S(1)}, f32[128,2048]{1,0:T(8,128)S(1)}, u32[]{:S(2)}, u32[]{:S(2)}) collective-permute-start(f32[128,2048]{1,0:T(8,128)S(1)} %widen_own.1.own), channel_id=1, source_target_pairs={{0,256},{256,0},{1,257},{257,1},{2,258},{258,2},{3,259},{259,3},{4... | collective-permute-start | bytes 3145736 | tf_op jit(solution)/shard_map/ppermute | solution.py:364

commit v7 on v6

--- a/solution.py
+++ b/solution.py
@@ -154,21 +154,21 @@
     def fold(value):
         return jnp.sum(value, axis=0, keepdims=True)
 
-    def send(chunk, row, vector):
-        for peer in range(4 * chunk, 4 * chunk + 4):
+    def send(row, vector):
+        for peer in range(8):
             sends[peer, row // 4, row % 4 : row % 4 + 1, :] = vector
 
     for tile in range(TILES_IN):
         plain, weighted = column(0, 0, tile)
-        send(tile // 8, tile % 8, fold(plain))
-        send(tile // 8, 8 + tile % 8, fold(weighted))
+        send(tile, fold(plain))
+        send(16 + tile, fold(weighted))
     for tile in range(TILES_OUT):
         plain, weighted = column(64, 64, tile)
         for k in range(1, BLOCKS):
             more = column(64, 64 + 64 * k, k * TILES_OUT + tile)
             plain, weighted = plain + more[0], weighted + more[1]
-        send(tile // 2, 16 + tile % 2, fold(plain))
-        send(tile // 2, 18 + tile % 2, fold(weighted))
+        send(32 + tile, fold(plain))
+        send(36 + tile, fold(weighted))
 
 
 def column_sums_of(row_sums, rows_in, rows_out, summed):
@@ -179,7 +179,7 @@
             jax.ShapeDtypeStruct((320, 128), F32),
             jax.ShapeDtypeStruct((1, ROWS_IN), F32),
             jax.ShapeDtypeStruct((1, ROWS_OUT), F32),
-            jax.ShapeDtypeStruct((8, 5, 4, 128), F32),
+            jax.ShapeDtypeStruct((8, 10, 4, 128), F32),
         ),
         in_specs=[VMEM] * 4,
         out_specs=(VMEM,) * 5,
@@ -199,7 +199,7 @@
 def total_of(sums):
     return pl.pallas_call(
         total_kernel,
-        out_shape=jax.ShapeDtypeStruct((8, 5, 4, 128), F32),
+        out_shape=jax.ShapeDtypeStruct((8, 10, 4, 128), F32),
         in_specs=[VMEM],
         out_specs=VMEM,
         compiler_params=PARAMS,
@@ -208,27 +208,28 @@
 
 
 def factors_kernel(sums, cols_in, cols_out, sends):
-    chunk = lax.axis_index("dp") * 2 + lax.axis_index("pair")
+    half = lax.axis_index("dp")
     total = sums[0]
     for peer in range(1, 8):
         total = total + sums[peer]
     energy_in = jnp.zeros((1, 128), F32)
-    for part in range(2):
-        new_in = DECAY * cols_in[chunk * 2 + part] + (1.0 - DECAY) * (total[part] * (1.0 / D) + EPSILON)
-        energy_in += jnp.sum(total[2 + part] / new_in, axis=0, keepdims=True)
-        for peer in range(16):
+    for part in range(4):
+        new_in = DECAY * cols_in[half * 4 + part] + (1.0 - DECAY) * (total[part] * (1.0 / D) + EPSILON)
+        energy_in += jnp.sum(total[4 + part] / new_in, axis=0, keepdims=True)
+        for peer in range(8):
             sends[peer, part] = new_in
-    new_out = DECAY * cols_out[chunk] + (1.0 - DECAY) * (total[4, 0:2] * (1.0 / FF) + EPSILON)
-    energy_out = jnp.sum(total[4, 2:4] / new_out, axis=0, keepdims=True)
-    last = jnp.concatenate([new_out, energy_in, energy_out], axis=0)
-    for peer in range(16):
-        sends[peer, 2] = last
+    new_out = DECAY * cols_out[half] + (1.0 - DECAY) * (total[8] * (1.0 / FF) + EPSILON)
+    energy_out = jnp.sum(total[9] / new_out, axis=0, keepdims=True)
+    last = jnp.concatenate([energy_in, energy_out, jnp.zeros((2, 128), F32)], axis=0)
+    for peer in range(8):
+        sends[peer, 4] = new_out
+        sends[peer, 5] = last
 
 
 def factors_of(sums, cols_in, cols_out):
     return pl.pallas_call(
         factors_kernel,
-        out_shape=jax.ShapeDtypeStruct((16, 3, 4, 128), F32),
+        out_shape=jax.ShapeDtypeStruct((8, 6, 4, 128), F32),
         in_specs=[VMEM] * 3,
         out_specs=VMEM,
         compiler_params=PARAMS,
@@ -238,24 +239,24 @@
 
 def scales_kernel(factors, cols, scales):
     my_x = lax.axis_index("x")
-    energies = factors[0, 2]
-    for peer in range(1, 16):
-        energies = energies + factors[peer, 2]
+    energies = factors[0, 5]
+    for peer in range(1, 8):
+        energies = energies + factors[peer, 5]
 
     def limit(row):
         energy = jnp.sum(energies[row : row + 1, :], axis=1, keepdims=True)
         return 1.0 / jnp.maximum(1.0, jnp.sqrt(energy * (1.0 / (D * FF))))
 
-    limit_in, limit_out = limit(2), limit(3)
-    for chunk in range(4):
-        owner = my_x * 4 + chunk % 2 * 2 + chunk // 2
-        for part in range(2):
+    limit_in, limit_out = limit(0), limit(1)
+    for half in range(2):
+        owner = my_x * 2 + half
+        for part in range(4):
             here = factors[owner, part]
-            cols[pl.ds(chunk * 8 + part * 4, 4), :] = here
-            scales[pl.ds(chunk * 8 + part * 4, 4), :] = lax.rsqrt(here) * limit_in
-        here = factors[owner, 2, 0:2, :]
-        cols[pl.ds(32 + chunk * 2, 2), :] = here
-        scales[pl.ds(32 + chunk * 2, 2), :] = lax.rsqrt(here) * limit_out
+            cols[pl.ds(half * 16 + part * 4, 4), :] = here
+            scales[pl.ds(half * 16 + part * 4, 4), :] = lax.rsqrt(here) * limit_in
+        here = factors[owner, 4]
+        cols[pl.ds(32 + half * 4, 4), :] = here
+        scales[pl.ds(32 + half * 4, 4), :] = lax.rsqrt(here) * limit_out
 
 
 def scales_of(factors):
@@ -355,7 +356,7 @@
                 rows_in.reshape(1, ROWS_IN),
                 rows_out.reshape(1, ROWS_OUT),
                 cols_in.reshape(8, 4, 128),
-                cols_out.reshape(4, 2, 128),
+                cols_out.reshape(2, 4, 128),
             ),
         )
     )
@@ -366,9 +367,9 @@
     summed, row_sums = row_sums_of(own, arrived_own)
     row_sums = lax.all_to_all(row_sums, ("x", "dp"), 0, 0)
     scaled, row_scale, new_rows_in, new_rows_out, sums = column_sums_of(row_sums, rows_in, rows_out, summed)
-    sums = lax.all_to_all(sums, ("pair", "y"), 0, 0)
+    sums = lax.all_to_all(sums, "y", 0, 0)
     sums = lax.all_to_all(total_of(sums), "z", 0, 0)
-    factors = lax.all_to_all(factors_of(sums, cols_in, cols_out), ("x", "pair", "dp"), 0, 0)
+    factors = lax.all_to_all(factors_of(sums, cols_in, cols_out), ("x", "dp"), 0, 0)
     cols, scales = scales_of(factors)
     update_in, update_out, new_rows_in, new_rows_out, new_cols_in, new_cols_out = update_of(
         cols, scales, scaled, row_scale, first, arrived_other, new_rows_in, new_rows_out
@@ -384,8 +385,8 @@
 
 
 def solution(mesh):
-    fine = Mesh(mesh.devices.reshape(2, 8, 4, 2, 4), ("dp", "z", "y", "pair", "x"))
-    row = ("z", "y", "pair")
+    fine = Mesh(mesh.devices.reshape(2, 8, 8, 4), ("dp", "z", "y", "x"))
+    row = ("z", "y")
     return jax.shard_map(
         per_device,
         mesh=fine,

time: 62.1 us -> 63.4 us (1.021)
  blocking collectives: 46.6 us -> 48 us
    all_to_all x1, blocking collectives: 17.2 us -> 18.1 us  [per_device(): sums = lax.all_to_all(total_of(sums), 'z', 0, 0)]
where the time goes in v7:
time: 63.4 us; the launch traced here: 63.1 us
  blocking collectives  48 us (76%)
  starting transfers between devices  10.7 us (17%)
  Pallas kernels  3.49 us (6%)
  between operations  0.73 us (1%)
    all_to_all x1, blocking collectives, per_device(): sums = lax.all_to_all(total_of(sums), 'z', 0, 0)  18.1 us
    all_to_all x1, blocking collectives, per_device(): lax.all_to_all(factors_of(sums, cols_in, cols_out), ('x', 'dp'), 0, 0)  11.4 us
    all_to_all x1, blocking collectives, per_device(): sums = lax.all_to_all(sums, 'y', 0, 0)  11.1 us
    ppermute x1, starting transfers between devices, per_device(): arrived_own = lax.ppermute(first, 'dp', swap)  8.79 us
    all_to_all x1, blocking collectives, per_device(): row_sums = lax.all_to_all(row_sums, ('x', 'dp'), 0, 0)  7.36 us
    ppermute x1, starting transfers between devices, per_device(): arrived_other = lax.ppermute(own, 'dp', swap)  1.92 us
    pallas_call x1, Pallas kernels, update_of(): pl.pallas_call(update_kernel, out_shape=(jax.ShapeDtypeStruct((ROWS_IN, C...  1.45 us
  transfers between devices with their start and end apart: 2, of which 1 were waited for; matrix products, arithmetic and copies ran while one was open for 0% of the time, Pallas kernels for 1%

profile of v7, /device:TPU:1, one launch (start us, length us, event | category | flops | bytes accessed | tf_op | source)
XLA Modules:
  0.0 63.1 jit_solution(973419295782274628)
XLA Ops:
  0.6 0.0 copy-start
  0.6 0.0 copy-start.1
  0.7 1.2 %fetch.1 = (f32[128,2048]{1,0:T(8,128)S(1)}, f32[1,64]{1,0:T(1,128)S(1)}, f32[1,256]{1,0:T(1,128)S(1)}, f32[8,4,128]{2,1,0:T(4,128)S(1)}, f32[2,4,128]{2,1,0:T(4,128)S(1)}) custom-call(bf16[64,4096]{1,0:T(8,128)(2,1)} %bitcast.10, bf16[256,1024]{1,0:T(8,128)(2,1)} %bitcast.12, f32[1,64]{1,0:T(1,128)} %bitcast.17, f32[1,256]{1,0:T(1,128)} %bitcast.16, ...), custom_call_target="tpu_custom_call" | custom-call | tf_op jit(solution)/shard_map/fetch/pallas_call | solution.py:63
  1.9 8.8 %collective-permute-start = (f32[128,2048]{1,0:T(8,128)S(1)}, f32[128,2048]{1,0:T(8,128)S(1)}, u32[]{:S(2)}, u32[]{:S(2)}) collective-permute-start(f32[128,2048]{1,0:T(8,128)S(1)} %get-tuple-element.26.first), channel_id=1, source_target_pairs={{0,256},{256,0},{1,257},{257,1},{2,258},{258,2},{3,259},{259,3},{4... | collective-permute-start | bytes 3145736 | tf_op jit(solution)/shard_map/ppermute | solution.py:363
  10.7 0.0 copy-done
  10.7 0.0 copy-done.1
  10.7 0.1 widen_own.1.own
  10.8 1.9 %collective-permute-start.1 = (f32[128,2048]{1,0:T(8,128)S(1)}, f32[128,2048]{1,0:T(8,128)S(1)}, u32[]{:S(2)}, u32[]{:S(2)}) collective-permute-start(f32[128,2048]{1,0:T(8,128)S(1)} %widen_own.1.own), channel_id=1, source_target_pairs={{0,256},{256,0},{1,257},{257,1},{2,258},{258,2},{3,259},{259,3},{4... | collective-permute-start | bytes 3145736 | tf_op jit(solution)/shard_map/ppermute | solution.py:365
  12.7 0.2 collective-permute-done.received
  12.9 0.2 row_sums.1
  13.2 7.4 %all_to_all.20.row_sums = f32[8,1,384]{2,1,0:T(1,128)S(1)} all-to-all(f32[8,1,384]{2,1,0:T(1,128)S(1)} %get-tuple-element.27), channel_id=1, replica_groups=mesh['dp'=2,'z'=8,'y'=8,'x'=4] {'x','dp'}, dimensions={0} | all-to-all | bytes 24576 | tf_op jit(solution)/shard_map/all_to_all | solution.py:368
  20.5 0.3 column_sums.1
  20.9 11.1 %all_to_all.21.sums = f32[8,10,4,128]{3,2,1,0:T(4,128)S(1)} all-to-all(f32[8,10,4,128]{3,2,1,0:T(4,128)S(1)} %get-tuple-element.31), channel_id=1, replica_groups=mesh['dp'=2,'z'=8,'y'=8,'x'=4] {'y'}, dimensions={0} | all-to-all | bytes 327680 | tf_op jit(solution)/shard_map/all_to_all | solution.py:370
  32.0 18.1 %all_to_all.22.sums = f32[8,10,4,128]{3,2,1,0:T(4,128)S(1)} all-to-all(f32[8,10,4,128]{3,2,1,0:T(4,128)S(1)} %total.1), channel_id=1, replica_groups=mesh['dp'=2,'z'=8,'y'=8,'x'=4] {'z'}, dimensions={0} | all-to-all | bytes 327680 | tf_op jit(solution)/shard_map/all_to_all | solution.py:371
  50.2 11.4 %all_to_all.23.factors = f32[8,6,4,128]{3,2,1,0:T(4,128)S(1)} all-to-all(f32[8,6,4,128]{3,2,1,0:T(4,128)S(1)} %column_factors.1), channel_id=1, replica_groups=mesh['dp'=2,'z'=8,'y'=8,'x'=4] {'x','dp'}, dimensions={0} | all-to-all | bytes 196608 | tf_op jit(solution)/shard_map/all_to_all | solution.py:372
  61.6 0.1 scales.1
  61.7 0.0 collective-permute-done.1.received
  61.7 1.4 %update.1 = (f32[64,4096]{1,0:T(8,128)}, f32[256,1024]{1,0:T(8,128)}, f32[1,64]{1,0:T(1,128)}, f32[1,256]{1,0:T(1,128)}, f32[32,128]{1,0:T(8,128)}, /*index=5*/f32[8,128]{1,0:T(8,128)}) custom-call(f32[40,128]{1,0:T(8,128)S(1)} %get-tuple-element.34.cols, f32[40,128]{1,0:T(8,128)S(1)} %get-tuple-element.35.scales, f32[128,2048]{1,0:T(8,128)S(1)} %get-tuple-element.36.scaled, ...), custom_call_target="tpu_custom_call" | custom-call | tf_op jit(solution)/shard_map/update/pallas_call | solution.py:321
  (2 shorter events, 0.1 us)
Async XLA Ops:
  0.6 10.0 %copy-start = (bf16[1,64,4096]{2,1,0:T(8,128)(2,1)S(1)}, bf16[1,64,4096]{2,1,0:T(8,128)(2,1)}, u32[]{:S(2)}) copy-start(bf16[1,64,4096]{2,1,0:T(8,128)(2,1)} %param.6) | copy-start | bytes 1572868
  0.6 10.0 %copy-start.1 = (bf16[1,256,1024]{2,1,0:T(8,128)(2,1)S(1)}, bf16[1,256,1024]{2,1,0:T(8,128)(2,1)}, u32[]{:S(2)}) copy-start(bf16[1,256,1024]{2,1,0:T(8,128)(2,1)} %param.7) | copy-start | bytes 1572868
  1.9 11.1 %collective-permute-start = (f32[128,2048]{1,0:T(8,128)S(1)}, f32[128,2048]{1,0:T(8,128)S(1)}, u32[]{:S(2)}, u32[]{:S(2)}) collective-permute-start(f32[128,2048]{1,0:T(8,128)S(1)} %get-tuple-element.26.first), channel_id=1, source_target_pairs={{0,256},{256,0},{1,257},{257,1},{2,258},{258,2},{3,259},{259,3},{4... | collective-permute-start | bytes 3145736 | tf_op jit(solution)/shard_map/ppermute | solution.py:363
  10.8 50.9 %collective-permute-start.1 = (f32[128,2048]{1,0:T(8,128)S(1)}, f32[128,2048]{1,0:T(8,128)S(1)}, u32[]{:S(2)}, u32[]{:S(2)}) collective-permute-start(f32[128,2048]{1,0:T(8,128)S(1)} %widen_own.1.own), channel_id=1, source_target_pairs={{0,256},{256,0},{1,257},{257,1},{2,258},{258,2},{3,259},{259,3},{4... | collective-permute-start | bytes 3145736 | tf_op jit(solution)/shard_map/ppermute | solution.py:365

commit v8 on v6

--- a/solution.py
+++ b/solution.py
@@ -45,10 +45,12 @@
 
 
 def fetch_kernel(grad_in, grad_out, *refs):
-    first, other_in, other_out, sems = refs[4], refs[9], refs[10], refs[11]
+    first, other_in, other_out, sems = refs[2], refs[5], refs[6], refs[7]
     copies = half_copies(grad_in, grad_out, 1 - lax.axis_index("dp"), other_in, other_out, sems)
-    small = [pltpu.make_async_copy(refs[at], refs[5 + at], sems.at[2 + at]) for at in range(4)]
-    for copy in (*copies, *small):
+    small = [pltpu.make_async_copy(refs[at], refs[3 + at], sems.at[2 + at]) for at in range(2)]
+    for copy in copies:
+        copy.start(priority=1)
+    for copy in small:
         copy.start()
     copies[0].wait()
     first[0:64, :] = other_in[...].astype(F32)
@@ -63,9 +65,9 @@
     return pl.pallas_call(
         fetch_kernel,
         out_shape=tuple(jax.ShapeDtypeStruct(shape, F32) for shape in (PACK, *(x.shape for x in factors))),
-        in_specs=[HBM] * 6,
-        out_specs=(VMEM,) * 5,
-        scratch_shapes=HALF_SCRATCH + [pltpu.SemaphoreType.DMA((6,))],
+        in_specs=[HBM] * 4,
+        out_specs=(VMEM,) * 3,
+        scratch_shapes=HALF_SCRATCH + [pltpu.SemaphoreType.DMA((4,))],
         compiler_params=PARAMS,
         name="fetch",
     )(grad_in, grad_out, *factors)
@@ -346,7 +348,7 @@
 def per_device(grad_in, grad_out, rows_in, cols_in, rows_out, cols_out):
     swap = [(0, 1), (1, 0)]
     grad_in, grad_out = grad_in[0], grad_out[0]
-    first, rows_in, rows_out, cols_in, cols_out = fetch(
+    first, rows_in, rows_out = fetch(
         *map(
             keep_in_hbm,
             (
@@ -354,8 +356,6 @@
                 grad_out,
                 rows_in.reshape(1, ROWS_IN),
                 rows_out.reshape(1, ROWS_OUT),
-                cols_in.reshape(8, 4, 128),
-                cols_out.reshape(4, 2, 128),
             ),
         )
     )
@@ -368,7 +368,8 @@
     scaled, row_scale, new_rows_in, new_rows_out, sums = column_sums_of(row_sums, rows_in, rows_out, summed)
     sums = lax.all_to_all(sums, ("pair", "y"), 0, 0)
     sums = lax.all_to_all(total_of(sums), "z", 0, 0)
-    factors = lax.all_to_all(factors_of(sums, cols_in, cols_out), ("x", "pair", "dp"), 0, 0)
+    factors = factors_of(sums, cols_in.reshape(8, 4, 128), cols_out.reshape(4, 2, 128))
+    factors = lax.all_to_all(factors, ("x", "pair", "dp"), 0, 0)
     cols, scales = scales_of(factors)
     update_in, update_out, new_rows_in, new_rows_out, new_cols_in, new_cols_out = update_of(
         cols, scales, scaled, row_scale, first, arrived_other, new_rows_in, new_rows_out

time: 62.1 us -> 62.2 us (level)
  no operation moved by 1% of the time
where the time goes in v8:
time: 62.2 us; the launch traced here: 61.8 us
  blocking collectives  46.6 us (75%)
  starting transfers between devices  10.7 us (17%)
  Pallas kernels  3.45 us (6%)
  between operations  0.74 us (1%)
    all_to_all x1, blocking collectives, per_device(): sums = lax.all_to_all(total_of(sums), 'z', 0, 0)  17.2 us
    all_to_all x1, blocking collectives, per_device(): factors = lax.all_to_all(factors, ('x', 'pair', 'dp'), 0, 0)  12.2 us
    all_to_all x1, blocking collectives, per_device(): sums = lax.all_to_all(sums, ('pair', 'y'), 0, 0)  9.8 us
    ppermute x1, starting transfers between devices, per_device(): arrived_own = lax.ppermute(first, 'dp', swap)  8.79 us
    all_to_all x1, blocking collectives, per_device(): row_sums = lax.all_to_all(row_sums, ('x', 'dp'), 0, 0)  7.36 us
    ppermute x1, starting transfers between devices, per_device(): arrived_other = lax.ppermute(own, 'dp', swap)  1.92 us
    pallas_call x1, Pallas kernels, update_of(): pl.pallas_call(update_kernel, out_shape=(jax.ShapeDtypeStruct((ROWS_IN, C...  1.45 us
  transfers between devices with their start and end apart: 2, of which 1 were waited for; matrix products, arithmetic and copies ran while one was open for 0% of the time, Pallas kernels for 1%

profile of v8, /device:TPU:1, one launch (start us, length us, event | category | flops | bytes accessed | tf_op | source)
XLA Modules:
  0.0 61.8 jit_solution(2924422953376349073)
XLA Ops:
  0.6 0.0 copy-start
  0.6 0.0 copy-start.1
  0.7 1.2 %fetch.1 = (f32[128,2048]{1,0:T(8,128)S(1)}, f32[1,64]{1,0:T(1,128)S(1)}, f32[1,256]{1,0:T(1,128)S(1)}) custom-call(bf16[64,4096]{1,0:T(8,128)(2,1)} %bitcast.10, bf16[256,1024]{1,0:T(8,128)(2,1)} %bitcast.12, f32[1,64]{1,0:T(1,128)} %bitcast.17, f32[1,256]{1,0:T(1,128)} %bitcast.16), custom_call_target="tpu_custom_call" | custom-call | tf_op jit(solution)/shard_map/fetch/pallas_call | solution.py:65
  1.9 8.8 %collective-permute-start = (f32[128,2048]{1,0:T(8,128)S(1)}, f32[128,2048]{1,0:T(8,128)S(1)}, u32[]{:S(2)}, u32[]{:S(2)}) collective-permute-start(f32[128,2048]{1,0:T(8,128)S(1)} %get-tuple-element.24.first), channel_id=1, source_target_pairs={{0,256},{256,0},{1,257},{257,1},{2,258},{258,2},{3,259},{259,3},{4... | collective-permute-start | bytes 3145736 | tf_op jit(solution)/shard_map/ppermute | solution.py:362
  10.7 0.0 copy-done
  10.7 0.0 copy-done.1
  10.7 0.1 widen_own.1.own
  10.8 1.9 %collective-permute-start.1 = (f32[128,2048]{1,0:T(8,128)S(1)}, f32[128,2048]{1,0:T(8,128)S(1)}, u32[]{:S(2)}, u32[]{:S(2)}) collective-permute-start(f32[128,2048]{1,0:T(8,128)S(1)} %widen_own.1.own), channel_id=1, source_target_pairs={{0,256},{256,0},{1,257},{257,1},{2,258},{258,2},{3,259},{259,3},{4... | collective-permute-start | bytes 3145736 | tf_op jit(solution)/shard_map/ppermute | solution.py:364
  12.7 0.2 collective-permute-done.received
  12.9 0.2 row_sums.1
  13.2 7.4 %all_to_all.20.row_sums = f32[8,1,384]{2,1,0:T(1,128)S(1)} all-to-all(f32[8,1,384]{2,1,0:T(1,128)S(1)} %get-tuple-element.25), channel_id=1, replica_groups=mesh['dp'=2,'z'=8,'y'=4,'pair'=2,'x'=4] {'x','dp'}, dimensions={0} | all-to-all | bytes 24576 | tf_op jit(solution)/shard_map/all_to_all | solution.py:367
  20.6 0.3 column_sums.1
  20.8 9.8 %all_to_all.21.sums = f32[8,5,4,128]{3,2,1,0:T(4,128)S(1)} all-to-all(f32[8,5,4,128]{3,2,1,0:T(4,128)S(1)} %get-tuple-element.29), channel_id=1, replica_groups=mesh['dp'=2,'z'=8,'y'=4,'pair'=2,'x'=4] {'pair','y'}, dimensions={0} | all-to-all | bytes 163840 | tf_op jit(solution)/shard_map/all_to_all | solution.py:369
  30.7 0.0 copy-start.2
  30.7 0.0 copy-start.3
  30.7 17.2 %all_to_all.22.sums = f32[8,5,4,128]{3,2,1,0:T(4,128)S(1)} all-to-all(f32[8,5,4,128]{3,2,1,0:T(4,128)S(1)} %total.1), channel_id=1, replica_groups=mesh['dp'=2,'z'=8,'y'=4,'pair'=2,'x'=4] {'z'}, dimensions={0} | all-to-all | bytes 163840 | tf_op jit(solution)/shard_map/all_to_all | solution.py:370
  47.9 0.0 copy-done.2
  47.9 0.0 copy-done.3
  48.0 12.2 %all_to_all.23.factors = f32[16,3,4,128]{3,2,1,0:T(4,128)S(1)} all-to-all(f32[16,3,4,128]{3,2,1,0:T(4,128)S(1)} %column_factors.1), channel_id=1, replica_groups=mesh['dp'=2,'z'=8,'y'=4,'pair'=2,'x'=4] {'x','pair','dp'}, dimensions={0} | all-to-all | bytes 196608 | tf_op jit(solution)/shard_map/all_to_all | solution.py:372
  60.2 0.1 scales.1
  60.3 0.0 collective-permute-done.1.received
  60.3 1.4 %update.1 = (f32[64,4096]{1,0:T(8,128)}, f32[256,1024]{1,0:T(8,128)}, f32[1,64]{1,0:T(1,128)}, f32[1,256]{1,0:T(1,128)}, f32[32,128]{1,0:T(8,128)}, /*index=5*/f32[8,128]{1,0:T(8,128)}) custom-call(f32[40,128]{1,0:T(8,128)S(1)} %get-tuple-element.30.cols, f32[40,128]{1,0:T(8,128)S(1)} %get-tuple-element.31.scales, f32[128,2048]{1,0:T(8,128)S(1)} %get-tuple-element.32.scaled, ...), custom_call_target="tpu_custom_call" | custom-call | tf_op jit(solution)/shard_map/update/pallas_call | solution.py:322
  (2 shorter events, 0.1 us)
Async XLA Ops:
  0.6 10.1 %copy-start = (bf16[1,64,4096]{2,1,0:T(8,128)(2,1)S(1)}, bf16[1,64,4096]{2,1,0:T(8,128)(2,1)}, u32[]{:S(2)}) copy-start(bf16[1,64,4096]{2,1,0:T(8,128)(2,1)} %param.6) | copy-start | bytes 1572868
  0.6 10.1 %copy-start.1 = (bf16[1,256,1024]{2,1,0:T(8,128)(2,1)S(1)}, bf16[1,256,1024]{2,1,0:T(8,128)(2,1)}, u32[]{:S(2)}) copy-start(bf16[1,256,1024]{2,1,0:T(8,128)(2,1)} %param.7) | copy-start | bytes 1572868
  1.9 11.1 %collective-permute-start = (f32[128,2048]{1,0:T(8,128)S(1)}, f32[128,2048]{1,0:T(8,128)S(1)}, u32[]{:S(2)}, u32[]{:S(2)}) collective-permute-start(f32[128,2048]{1,0:T(8,128)S(1)} %get-tuple-element.24.first), channel_id=1, source_target_pairs={{0,256},{256,0},{1,257},{257,1},{2,258},{258,2},{3,259},{259,3},{4... | collective-permute-start | bytes 3145736 | tf_op jit(solution)/shard_map/ppermute | solution.py:362
  10.8 49.5 %collective-permute-start.1 = (f32[128,2048]{1,0:T(8,128)S(1)}, f32[128,2048]{1,0:T(8,128)S(1)}, u32[]{:S(2)}, u32[]{:S(2)}) collective-permute-start(f32[128,2048]{1,0:T(8,128)S(1)} %widen_own.1.own), channel_id=1, source_target_pairs={{0,256},{256,0},{1,257},{257,1},{2,258},{258,2},{3,259},{259,3},{4... | collective-permute-start | bytes 3145736 | tf_op jit(solution)/shard_map/ppermute | solution.py:364
  30.7 17.3 %copy-start.2 = (f32[4096]{0:T(1024)S(1)}, f32[4096]{0:T(1024)}, u32[]{:S(2)}) copy-start(f32[4096]{0:T(1024)} %param.9) | copy-start | bytes 49156
  30.7 17.3 %copy-start.3 = (f32[1024]{0:T(1024)S(1)}, f32[1024]{0:T(1024)}, u32[]{:S(2)}) copy-start(f32[1024]{0:T(1024)} %param.11) | copy-start | bytes 12292

commit v9 on v6

--- a/solution.py
+++ b/solution.py
@@ -192,14 +192,18 @@
     total = sums[0]
     for peer in range(1, 8):
         total = total + sums[peer]
-    for peer in range(8):
-        sends[peer] = total
+    for quarter in range(2):
+        rest = jnp.concatenate([total[4, quarter : quarter + 1], total[4, 2 + quarter : 3 + quarter]], axis=0)
+        for peer in range(4 * quarter, 4 * quarter + 4):
+            sends[peer, 0] = total[quarter]
+            sends[peer, 1] = total[2 + quarter]
+            sends[peer, 2] = jnp.concatenate([rest, rest], axis=0)
 
 
 def total_of(sums):
     return pl.pallas_call(
         total_kernel,
-        out_shape=jax.ShapeDtypeStruct((8, 5, 4, 128), F32),
+        out_shape=jax.ShapeDtypeStruct((8, 3, 4, 128), F32),
         in_specs=[VMEM],
         out_specs=VMEM,
         compiler_params=PARAMS,
@@ -208,27 +212,24 @@
 
 
 def factors_kernel(sums, cols_in, cols_out, sends):
-    chunk = lax.axis_index("dp") * 2 + lax.axis_index("pair")
+    chunk = (lax.axis_index("dp") * 2 + lax.axis_index("zpair")) * 2 + lax.axis_index("ypair")
     total = sums[0]
     for peer in range(1, 8):
         total = total + sums[peer]
-    energy_in = jnp.zeros((1, 128), F32)
-    for part in range(2):
-        new_in = DECAY * cols_in[chunk * 2 + part] + (1.0 - DECAY) * (total[part] * (1.0 / D) + EPSILON)
-        energy_in += jnp.sum(total[2 + part] / new_in, axis=0, keepdims=True)
-        for peer in range(16):
-            sends[peer, part] = new_in
-    new_out = DECAY * cols_out[chunk] + (1.0 - DECAY) * (total[4, 0:2] * (1.0 / FF) + EPSILON)
-    energy_out = jnp.sum(total[4, 2:4] / new_out, axis=0, keepdims=True)
-    last = jnp.concatenate([new_out, energy_in, energy_out], axis=0)
-    for peer in range(16):
-        sends[peer, 2] = last
+    new_in = DECAY * cols_in[chunk] + (1.0 - DECAY) * (total[0] * (1.0 / D) + EPSILON)
+    energy_in = jnp.sum(total[1] / new_in, axis=0, keepdims=True)
+    new_out = DECAY * cols_out[chunk] + (1.0 - DECAY) * (total[2, 0:1] * (1.0 / FF) + EPSILON)
+    energy_out = total[2, 1:2] / new_out
+    last = jnp.concatenate([new_out, energy_in, energy_out, jnp.zeros((1, 128), F32)], axis=0)
+    for peer in range(32):
+        sends[peer, 0] = new_in
+        sends[peer, 1] = last
 
 
 def factors_of(sums, cols_in, cols_out):
     return pl.pallas_call(
         factors_kernel,
-        out_shape=jax.ShapeDtypeStruct((16, 3, 4, 128), F32),
+        out_shape=jax.ShapeDtypeStruct((32, 2, 4, 128), F32),
         in_specs=[VMEM] * 3,
         out_specs=VMEM,
         compiler_params=PARAMS,
@@ -238,24 +239,23 @@
 
 def scales_kernel(factors, cols, scales):
     my_x = lax.axis_index("x")
-    energies = factors[0, 2]
-    for peer in range(1, 16):
-        energies = energies + factors[peer, 2]
+    energies = factors[0, 1]
+    for peer in range(1, 32):
+        energies = energies + factors[peer, 1]
 
     def limit(row):
         energy = jnp.sum(energies[row : row + 1, :], axis=1, keepdims=True)
         return 1.0 / jnp.maximum(1.0, jnp.sqrt(energy * (1.0 / (D * FF))))
 
-    limit_in, limit_out = limit(2), limit(3)
-    for chunk in range(4):
-        owner = my_x * 4 + chunk % 2 * 2 + chunk // 2
-        for part in range(2):
-            here = factors[owner, part]
-            cols[pl.ds(chunk * 8 + part * 4, 4), :] = here
-            scales[pl.ds(chunk * 8 + part * 4, 4), :] = lax.rsqrt(here) * limit_in
-        here = factors[owner, 2, 0:2, :]
-        cols[pl.ds(32 + chunk * 2, 2), :] = here
-        scales[pl.ds(32 + chunk * 2, 2), :] = lax.rsqrt(here) * limit_out
+    limit_in, limit_out = limit(1), limit(2)
+    for chunk in range(8):
+        owner = my_x * 8 + chunk % 4 * 2 + chunk // 4
+        here = factors[owner, 0]
+        cols[pl.ds(chunk * 4, 4), :] = here
+        scales[pl.ds(chunk * 4, 4), :] = lax.rsqrt(here) * limit_in
+        here = factors[owner, 1, 0:1, :]
+        cols[pl.ds(32 + chunk, 1), :] = here
+        scales[pl.ds(32 + chunk, 1), :] = lax.rsqrt(here) * limit_out
 
 
 def scales_of(factors):
@@ -355,7 +355,7 @@
                 rows_in.reshape(1, ROWS_IN),
                 rows_out.reshape(1, ROWS_OUT),
                 cols_in.reshape(8, 4, 128),
-                cols_out.reshape(4, 2, 128),
+                cols_out.reshape(8, 1, 128),
             ),
         )
     )
@@ -366,9 +366,9 @@
     summed, row_sums = row_sums_of(own, arrived_own)
     row_sums = lax.all_to_all(row_sums, ("x", "dp"), 0, 0)
     scaled, row_scale, new_rows_in, new_rows_out, sums = column_sums_of(row_sums, rows_in, rows_out, summed)
-    sums = lax.all_to_all(sums, ("pair", "y"), 0, 0)
-    sums = lax.all_to_all(total_of(sums), "z", 0, 0)
-    factors = lax.all_to_all(factors_of(sums, cols_in, cols_out), ("x", "pair", "dp"), 0, 0)
+    sums = lax.all_to_all(sums, ("zpair", "z"), 0, 0)
+    sums = lax.all_to_all(total_of(sums), ("ypair", "y"), 0, 0)
+    factors = lax.all_to_all(factors_of(sums, cols_in, cols_out), ("x", "zpair", "ypair", "dp"), 0, 0)
     cols, scales = scales_of(factors)
     update_in, update_out, new_rows_in, new_rows_out, new_cols_in, new_cols_out = update_of(
         cols, scales, scaled, row_scale, first, arrived_other, new_rows_in, new_rows_out
@@ -384,8 +384,8 @@
 
 
 def solution(mesh):
-    fine = Mesh(mesh.devices.reshape(2, 8, 4, 2, 4), ("dp", "z", "y", "pair", "x"))
-    row = ("z", "y", "pair")
+    fine = Mesh(mesh.devices.reshape(2, 4, 2, 4, 2, 4), ("dp", "z", "zpair", "y", "ypair", "x"))
+    row = ("z", "zpair", "y", "ypair")
     return jax.shard_map(
         per_device,
         mesh=fine,

time: 62.1 us -> 63.3 us (1.019)
  blocking collectives: 46.6 us -> 47.8 us
    all_to_all x3, blocking collectives: 39.3 us -> 40.5 us  [the longest x1 14.1 us: per_device(): lax.all_to_all(factors_of(sums, cols_in, cols_out), ('x', 'zpair', 'ypair...]
where the time goes in v9:
time: 63.3 us; the launch traced here: 63 us
  blocking collectives  47.8 us (76%)
  starting transfers between devices  10.7 us (17%)
  Pallas kernels  3.46 us (5%)
  between operations  0.73 us (1%)
    all_to_all x1, blocking collectives, per_device(): lax.all_to_all(factors_of(sums, cols_in, cols_out), ('x', 'zpair', 'ypair...  14.1 us
    all_to_all x1, blocking collectives, per_device(): sums = lax.all_to_all(total_of(sums), ('ypair', 'y'), 0, 0)  13.3 us
    all_to_all x1, blocking collectives, per_device(): sums = lax.all_to_all(sums, ('zpair', 'z'), 0, 0)  13 us
    ppermute x1, starting transfers between devices, per_device(): arrived_own = lax.ppermute(first, 'dp', swap)  8.79 us
    all_to_all x1, blocking collectives, per_device(): row_sums = lax.all_to_all(row_sums, ('x', 'dp'), 0, 0)  7.36 us
    ppermute x1, starting transfers between devices, per_device(): arrived_other = lax.ppermute(own, 'dp', swap)  1.92 us
    pallas_call x1, Pallas kernels, update_of(): pl.pallas_call(update_kernel, out_shape=(jax.ShapeDtypeStruct((ROWS_IN, C...  1.45 us
  transfers between devices with their start and end apart: 2, of which 1 were waited for; matrix products, arithmetic and copies ran while one was open for 0% of the time, Pallas kernels for 1%

profile of v9, /device:TPU:1, one launch (start us, length us, event | category | flops | bytes accessed | tf_op | source)
XLA Modules:
  0.0 63.0 jit_solution(5908547347757971198)
XLA Ops:
  0.6 0.0 copy-start
  0.6 0.0 copy-start.1
  0.7 1.2 %fetch.1 = (f32[128,2048]{1,0:T(8,128)S(1)}, f32[1,64]{1,0:T(1,128)S(1)}, f32[1,256]{1,0:T(1,128)S(1)}, f32[8,4,128]{2,1,0:T(4,128)S(1)}, f32[8,1,128]{2,1,0:T(1,128)S(1)}) custom-call(bf16[64,4096]{1,0:T(8,128)(2,1)} %bitcast.10, bf16[256,1024]{1,0:T(8,128)(2,1)} %bitcast.12, f32[1,64]{1,0:T(1,128)} %bitcast.17, f32[1,256]{1,0:T(1,128)} %bitcast.16, ...), custom_call_target="tpu_custom_call" | custom-call | tf_op jit(solution)/shard_map/fetch/pallas_call | solution.py:63
  1.9 8.8 %collective-permute-start = (f32[128,2048]{1,0:T(8,128)S(1)}, f32[128,2048]{1,0:T(8,128)S(1)}, u32[]{:S(2)}, u32[]{:S(2)}) collective-permute-start(f32[128,2048]{1,0:T(8,128)S(1)} %get-tuple-element.26.first), channel_id=1, source_target_pairs={{0,256},{256,0},{1,257},{257,1},{2,258},{258,2},{3,259},{259,3},{4... | collective-permute-start | bytes 3145736 | tf_op jit(solution)/shard_map/ppermute | solution.py:362
  10.7 0.0 copy-done
  10.7 0.0 copy-done.1
  10.7 0.1 widen_own.1.own
  10.8 1.9 %collective-permute-start.1 = (f32[128,2048]{1,0:T(8,128)S(1)}, f32[128,2048]{1,0:T(8,128)S(1)}, u32[]{:S(2)}, u32[]{:S(2)}) collective-permute-start(f32[128,2048]{1,0:T(8,128)S(1)} %widen_own.1.own), channel_id=1, source_target_pairs={{0,256},{256,0},{1,257},{257,1},{2,258},{258,2},{3,259},{259,3},{4... | collective-permute-start | bytes 3145736 | tf_op jit(solution)/shard_map/ppermute | solution.py:364
  12.7 0.2 collective-permute-done.received
  12.9 0.2 row_sums.1
  13.2 7.4 %all_to_all.20.row_sums = f32[8,1,384]{2,1,0:T(1,128)S(1)} all-to-all(f32[8,1,384]{2,1,0:T(1,128)S(1)} %get-tuple-element.27), channel_id=1, replica_groups=mesh['dp'=2,'z'=4,'zpair'=2,'y'=4,'ypair'=2,'x'=4] {'x','dp'}, dimensions={0} | all-to-all | bytes 24576 | tf_op jit(solution)/shard_map/all_to_all | solution.py:367
  20.5 0.3 column_sums.1
  20.8 13.0 %all_to_all.21.sums = f32[8,5,4,128]{3,2,1,0:T(4,128)S(1)} all-to-all(f32[8,5,4,128]{3,2,1,0:T(4,128)S(1)} %get-tuple-element.31), channel_id=1, replica_groups=mesh['dp'=2,'z'=4,'zpair'=2,'y'=4,'ypair'=2,'x'=4] {'zpair','z'}, dimensions={0} | all-to-all | bytes 163840 | tf_op jit(solution)/shard_map/all_to_all | solution.py:369
  33.9 13.3 %all_to_all.22.sums = f32[8,3,4,128]{3,2,1,0:T(4,128)S(1)} all-to-all(f32[8,3,4,128]{3,2,1,0:T(4,128)S(1)} %total.1), channel_id=1, replica_groups=mesh['dp'=2,'z'=4,'zpair'=2,'y'=4,'ypair'=2,'x'=4] {'ypair','y'}, dimensions={0} | all-to-all | bytes 98304 | tf_op jit(solution)/shard_map/all_to_all | solution.py:370
  47.2 14.1 %all_to_all.23.factors = f32[32,2,4,128]{3,2,1,0:T(4,128)S(1)} all-to-all(f32[32,2,4,128]{3,2,1,0:T(4,128)S(1)} %column_factors.1), channel_id=1, replica_groups=mesh['dp'=2,'z'=4,'zpair'=2,'y'=4,'ypair'=2,'x'=4] {'x','zpair','ypair',..., dimensions={0} | all-to-all | bytes 262144 | tf_op jit(solution)/shard_map/all_to_all | solution.py:371
  61.4 0.1 scales.1
  61.5 0.0 collective-permute-done.1.received
  61.5 1.4 %update.1 = (f32[64,4096]{1,0:T(8,128)}, f32[256,1024]{1,0:T(8,128)}, f32[1,64]{1,0:T(1,128)}, f32[1,256]{1,0:T(1,128)}, f32[32,128]{1,0:T(8,128)}, /*index=5*/f32[8,128]{1,0:T(8,128)}) custom-call(f32[40,128]{1,0:T(8,128)S(1)} %get-tuple-element.34.cols, f32[40,128]{1,0:T(8,128)S(1)} %get-tuple-element.35.scales, f32[128,2048]{1,0:T(8,128)S(1)} %get-tuple-element.36.scaled, ...), custom_call_target="tpu_custom_call" | custom-call | tf_op jit(solution)/shard_map/update/pallas_call | solution.py:320
  (2 shorter events, 0.1 us)
Async XLA Ops:
  0.6 10.0 %copy-start = (bf16[1,64,4096]{2,1,0:T(8,128)(2,1)S(1)}, bf16[1,64,4096]{2,1,0:T(8,128)(2,1)}, u32[]{:S(2)}) copy-start(bf16[1,64,4096]{2,1,0:T(8,128)(2,1)} %param.6) | copy-start | bytes 1572868
  0.6 10.0 %copy-start.1 = (bf16[1,256,1024]{2,1,0:T(8,128)(2,1)S(1)}, bf16[1,256,1024]{2,1,0:T(8,128)(2,1)}, u32[]{:S(2)}) copy-start(bf16[1,256,1024]{2,1,0:T(8,128)(2,1)} %param.7) | copy-start | bytes 1572868
  1.9 11.1 %collective-permute-start = (f32[128,2048]{1,0:T(8,128)S(1)}, f32[128,2048]{1,0:T(8,128)S(1)}, u32[]{:S(2)}, u32[]{:S(2)}) collective-permute-start(f32[128,2048]{1,0:T(8,128)S(1)} %get-tuple-element.26.first), channel_id=1, source_target_pairs={{0,256},{256,0},{1,257},{257,1},{2,258},{258,2},{3,259},{259,3},{4... | collective-permute-start | bytes 3145736 | tf_op jit(solution)/shard_map/ppermute | solution.py:362
  10.8 50.7 %collective-permute-start.1 = (f32[128,2048]{1,0:T(8,128)S(1)}, f32[128,2048]{1,0:T(8,128)S(1)}, u32[]{:S(2)}, u32[]{:S(2)}) collective-permute-start(f32[128,2048]{1,0:T(8,128)S(1)} %widen_own.1.own), channel_id=1, source_target_pairs={{0,256},{256,0},{1,257},{257,1},{2,258},{258,2},{3,259},{259,3},{4... | collective-permute-start | bytes 3145736 | tf_op jit(solution)/shard_map/ppermute | solution.py:364
